TPU v7x, 512 devices: a whole 4x8x8 slice. The times are simulated.
512 devices in a mesh: dp: 2 (over core), ctx: 32 (over x, z), tp: 8 (over y).
Axes of the slice: x: 4, y: 8, z: 8, core: 2. Of those that a mesh axis runs over, the one named last changes fastest.
Arguments:
- reception_entries: bfloat16 [2, 4096, 2048], P('dp', 'ctx', 'tp'), may hold values from -0.75 to 0.75
- address_entries: bfloat16 [2, 4096, 2048], P('dp', 'ctx', 'tp'), may hold values from -0.1796875 to 0.1796875
- payload_entries: bfloat16 [2, 4096, 2048], P('dp', 'ctx', 'tp'), may hold values from -6 to 6
- minus_logarithm_fade: float32 [2, 4096, 2048], P('dp', 'ctx', 'tp'), may hold values from 0 to 1, as said below
- erasure_axis: bfloat16 [2, 4096, 2048], P('dp', 'ctx', 'tp'), may hold values from -1 to 1, as said below
- inline_step_size: bfloat16 [2, 4096, 2048], P('dp', 'ctx', 'tp'), may hold values from 0.0029907227 to 0.29882812
- current_extra_scale: float32 [2048], P('tp'), may hold values from -8 to 8
- emitted_adjoint: bfloat16 [2, 4096, 2048], P('dp', 'ctx', 'tp'), may hold values from -6 to 6
Outputs:
- grad_receptance: bfloat16 [2, 4096, 2048], P('dp', 'ctx', 'tp')
- grad_key: bfloat16 [2, 4096, 2048], P('dp', 'ctx', 'tp')
- grad_value: bfloat16 [2, 4096, 2048], P('dp', 'ctx', 'tp')
- grad_decay: bfloat16 [2, 4096, 2048], P('dp', 'ctx', 'tp')
- grad_kappa: bfloat16 [2, 4096, 2048], P('dp', 'ctx', 'tp')
- grad_rate: bfloat16 [2, 4096, 2048], P('dp', 'ctx', 'tp')
- grad_bonus: float32 [2048], P('tp')
Inputs may be any that keep to these rules, and one draw needn't show every extreme that they name: `minus_logarithm_fade`: Positive. `erasure_axis`: each head's 64 entries at a token have unit Euclidean norm up to bfloat16 rounding.
All inputs are finite; a program needn't handle non-finite values.
Results may differ from a plain program's by a relative error of at most 0.0023.
Values sent between devices are 32-bit elements; how exact they have to be, the bound alone decides.
A program may use at most 128 MiB of HBM per device.

v0:
```python
import jax
import jax.numpy as jnp
from jax import lax
from jax.sharding import PartitionSpec as P

LANES_PER_GROUP = 64
SPAN = 64


def passed_along(value, axis, by):
    devices = lax.axis_size(axis)
    pairs = [(i, i + by) for i in range(devices) if 0 <= i + by < devices]
    return lax.ppermute(value, axis, pairs)


def matmul_hp(form, left, right):
    return jnp.einsum(form, left, right, precision=lax.Precision.HIGHEST)


def unit_lower_inverse(strict_part):
    length_here = strict_part.shape[-1]
    series = jnp.eye(length_here, dtype=jnp.float32) + strict_part
    raised = strict_part
    reached = 2
    while reached < length_here:
        raised = matmul_hp("bij,bjk->bik", raised, raised)
        series = series + matmul_hp("bij,bjk->bik", series, raised)
        reached = reached * 2
    return series


def segment_sweep(carried_matrix, stretch_cuts, extra_lines):
    (
        reception_lines,
        address_lines,
        value_row_list,
        decay_row_list,
        removal_rows,
        learning_rate_rows,
    ) = stretch_cuts
    length_here = reception_lines.shape[1]
    head_width = reception_lines.shape[2]
    row_ids = lax.broadcasted_iota(jnp.int32, (length_here, length_here), 0)
    col_ids = lax.broadcasted_iota(jnp.int32, (length_here, length_here), 1)
    strict = row_ids > col_ids
    inclusive = row_ids >= col_ids
    remove = -removal_rows
    writes = removal_rows * learning_rate_rows
    cumulative = jnp.cumsum(decay_row_list, axis=1)
    before = cumulative - decay_row_list
    middle = cumulative[:, length_here // 2 : length_here // 2 + 1, :]
    ending = cumulative[:, length_here - 1 : length_here, :]
    a_scaled = remove * jnp.exp(middle - before)
    b_scaled = writes * jnp.exp(cumulative - middle)
    k_scaled = address_lines * jnp.exp(cumulative - middle)
    r_scaled = reception_lines * jnp.exp(middle - cumulative)
    a_start = remove * jnp.exp(-before)
    r_start = reception_lines * jnp.exp(-cumulative)
    b_final = writes * jnp.exp(cumulative - ending)
    k_final = address_lines * jnp.exp(cumulative - ending)
    lower_write = jnp.where(strict, matmul_hp("btk,bsk->bts", a_scaled, b_scaled), 0.0)
    lower_key = jnp.where(strict, matmul_hp("btk,bsk->bts", a_scaled, k_scaled), 0.0)
    solved = unit_lower_inverse(lower_write)
    removed = matmul_hp(
        "bts,bsv->btv",
        solved,
        matmul_hp("btk,bvk->btv", a_start, carried_matrix)
        + matmul_hp("bts,bsv->btv", lower_key, value_row_list),
    )
    weigh_write = jnp.where(inclusive, matmul_hp("btk,bsk->bts", r_scaled, b_scaled), 0.0)
    weigh_key = jnp.where(inclusive, matmul_hp("btk,bsk->bts", r_scaled, k_scaled), 0.0)
    extra_share = (
        jnp.sum(reception_lines * extra_lines[:, None, :] * address_lines, axis=2, keepdims=True)
        * value_row_list
    )
    emitted_entry = (
        matmul_hp("btk,bvk->btv", r_start, carried_matrix)
        + matmul_hp("bts,bsv->btv", weigh_write, removed)
        + matmul_hp("bts,bsv->btv", weigh_key, value_row_list)
        + extra_share
    )
    updated_memory = (
        carried_matrix * jnp.exp(-ending)
        + matmul_hp("bsv,bsk->bvk", removed, b_final)
        + matmul_hp("bsv,bsk->bvk", value_row_list, k_final)
    )
    carried = matmul_hp("btk,bst->bks", a_start, solved)
    transfer_matrix = jnp.eye(head_width, dtype=jnp.float32) * jnp.exp(-ending) + matmul_hp(
        "bks,bsj->bkj", carried, b_final
    )
    return (updated_memory, emitted_entry, transfer_matrix)


def handle_segments(carried_matrix, stretch_parts, extra_lines):
    identity = jnp.broadcast_to(
        jnp.eye(carried_matrix.shape[-1], dtype=jnp.float32), carried_matrix.shape
    )

    def advance(carried_summary, stretch_cuts):
        updated_memory, emitted_entry, transfer_matrix = segment_sweep(
            carried_summary[0], stretch_cuts, extra_lines
        )
        return (
            (updated_memory, matmul_hp("bij,bjk->bik", carried_summary[1], transfer_matrix)),
            emitted_entry,
        )

    (last_memory_state, matrix_product), output_collection = lax.scan(
        advance, (carried_matrix, identity), stretch_parts
    )
    return (output_collection, last_memory_state, matrix_product)


def local(
    reception_entries,
    address_entries,
    payload_entries,
    minus_logarithm_fade,
    erasure_axis,
    inline_step_size,
    current_extra_scale,
    emitted_adjoint,
):
    shard_streams_py, tok_here, width_here = reception_entries.shape
    attention_groups_py = width_here // LANES_PER_GROUP
    blocks = tok_here // SPAN

    def to_local(values):
        shaped = values.astype(jnp.float32).reshape(
            shard_streams_py, blocks, SPAN, attention_groups_py, LANES_PER_GROUP
        )
        return shaped.transpose(1, 0, 3, 2, 4).reshape(
            blocks, shard_streams_py * attention_groups_py, SPAN, LANES_PER_GROUP
        )

    def to_global(values, dtype):
        shaped = values.reshape(
            blocks, shard_streams_py, attention_groups_py, SPAN, LANES_PER_GROUP
        ).transpose(1, 0, 3, 2, 4)
        return shaped.reshape(shard_streams_py, tok_here, width_here).astype(dtype)

    def break_lines(extra_scale):
        return jnp.tile(
            extra_scale.reshape(1, attention_groups_py, LANES_PER_GROUP), (shard_streams_py, 1, 1)
        ).reshape(shard_streams_py * attention_groups_py, LANES_PER_GROUP)

    stretch_parts = tuple(
        (
            to_local(argument_tensor)
            for argument_tensor in (
                reception_entries,
                address_entries,
                payload_entries,
                minus_logarithm_fade,
                erasure_axis,
                inline_step_size,
            )
        )
    )
    cotangent = to_local(emitted_adjoint)
    extra_lines = break_lines(current_extra_scale)
    empty = jnp.zeros(
        (shard_streams_py * attention_groups_py, LANES_PER_GROUP, LANES_PER_GROUP), jnp.float32
    )

    def from_state(carried_matrix):
        output_collection, last_memory_state, matrix_product = handle_segments(
            carried_matrix, stretch_parts, extra_lines
        )
        return ((output_collection, last_memory_state), matrix_product)

    first_results, pull_state, transfer_matrix = jax.vjp(from_state, empty, has_aux=True)
    local_state = first_results[1]
    local_adjoint = pull_state((cotangent, empty))[0]
    transposed = jnp.swapaxes(transfer_matrix, 1, 2)

    def relay_once(passed, carried_summary):
        state_out, adjoint_out, incoming, arriving = carried_summary
        incoming = passed_along(state_out, "ctx", 1)
        arriving = passed_along(adjoint_out, "ctx", -1)
        return (
            matmul_hp("bij,bjk->bik", incoming, transfer_matrix) + local_state,
            matmul_hp("bij,bjk->bik", arriving, transposed) + local_adjoint,
            incoming,
            arriving,
        )

    relayed = lax.fori_loop(
        0, lax.axis_size("ctx") - 1, relay_once, (local_state, local_adjoint, empty, empty)
    )
    start_state = relayed[2]
    end_adjoint = relayed[3]

    def complete_sweep(
        reception_lines,
        address_lines,
        value_row_list,
        decay_row_list,
        removal_rows,
        learning_rate_rows,
        extra_scale,
    ):
        output_collection, last_memory_state, unused = handle_segments(
            start_state,
            (
                reception_lines,
                address_lines,
                value_row_list,
                decay_row_list,
                removal_rows,
                learning_rate_rows,
            ),
            break_lines(extra_scale),
        )
        return (output_collection, last_memory_state)

    primal_result, pullback_function = jax.vjp(complete_sweep, *stretch_parts, current_extra_scale)
    derivative_outcomes = pullback_function((cotangent, end_adjoint))
    extra_summed = lax.psum(derivative_outcomes[6], ("dp", "ctx"))
    return (
        to_global(derivative_outcomes[0], jnp.bfloat16),
        to_global(derivative_outcomes[1], jnp.bfloat16),
        to_global(derivative_outcomes[2], jnp.bfloat16),
        to_global(derivative_outcomes[3], jnp.bfloat16),
        to_global(derivative_outcomes[4], jnp.bfloat16),
        to_global(derivative_outcomes[5], jnp.bfloat16),
        extra_summed,
    )


def solution(mesh):
    return jax.shard_map(
        local,
        mesh=mesh,
        in_specs=(
            P("dp", "ctx", "tp"),
            P("dp", "ctx", "tp"),
            P("dp", "ctx", "tp"),
            P("dp", "ctx", "tp"),
            P("dp", "ctx", "tp"),
            P("dp", "ctx", "tp"),
            P("tp"),
            P("dp", "ctx", "tp"),
        ),
        out_specs=(
            P("dp", "ctx", "tp"),
            P("dp", "ctx", "tp"),
            P("dp", "ctx", "tp"),
            P("dp", "ctx", "tp"),
            P("dp", "ctx", "tp"),
            P("dp", "ctx", "tp"),
            P("tp"),
        ),
        check_vma=False,
    )
```

profile of v0, /device:TPU:56, one launch (start us, length us, event | category | flops | bytes accessed | tf_op | source)
XLA Modules:
  0.0 688.8 jit_solution(13284071004765894971)
XLA Ops:
  8.5 19.2 %while.185 = (s32[]{:T(128)}, f32[4,64,64]{2,1,0:T(8,128)S(1)}, f32[4,64,64]{1,2,0:T(8,128)S(1)}, f32[2,4,64,64]{3,2,1,0:T(8,128)S(1)}, f32[2,4,64,64]{3,2,1,0:T...) while((s32[]{:T(128)}, f32[4,64,64]{2,1,0:T(8,128)S(1)}, ...), condition=%wide.region_2.3_spmd.clone.clone, body=%wide.region_0.2_spmd.clone.clone.sunk | while | flops 266133760 | bytes 10658128 | solution.py:108
  27.9 5.7 while.184
  33.8 365.1 %while.182 = (s32[]{:T(128)}, f32[4,64,64]{2,1,0:T(8,128)S(1)}, f32[4,64,64]{2,1,0:T(8,128)S(1)}, f32[4,64,64]{2,1,0:T(8,128)}, f32[4,64,64]{2,1,0:T(8,128)}, /*...) while((s32[]{:T(128)}, f32[4,64,64]{2,1,0:T(8,128)S(1)}, ...), condition=%wide.region_6.7_spmd, body=%wide.region_5.6_spmd.sunk | while | flops 25198592 | bytes 1573101 | solution.py:188
  33.9 4.3 collective-permute-start
  41.5 4.1 collective-permute-done.1
  46.3 4.3 collective-permute-start
  53.7 5.3 collective-permute-done.1
  59.7 4.9 collective-permute-start
  124.3 4.0 collective-permute-done.1
  153.0 4.1 collective-permute-start
  176.2 4.2 collective-permute-start
  210.8 4.0 collective-permute-start
  222.3 4.0 collective-permute-start
  234.0 4.0 collective-permute-start
  247.1 4.0 collective-permute-start
  281.5 4.2 collective-permute-start
  304.8 4.1 collective-permute-start
  316.5 4.0 collective-permute-start
  347.4 4.1 collective-permute-done.1
  364.3 4.0 collective-permute-start
  387.1 4.3 collective-permute-start
  423.2 39.5 %while.183 = (s32[]{:T(128)}, f32[4,64,64]{2,1,0:T(8,128)S(1)}, f32[2,4,64,64]{3,2,1,0:T(8,128)}, f32[2,4,64,64]{3,2,1,0:T(8,128)}, f32[2,4,64,64]{3,2,1,0:T(8,1...) while((s32[]{:T(128)}, f32[4,64,64]{2,1,0:T(8,128)S(1)}, ...), condition=%wide.region_10.11_spmd.clone.clone, body=%wide.region_7.10_spmd.clone.clone.sunk | while | flops 241229824 | bytes 38935856 | solution.py:108
  466.3 89.7 %while.186 = (s32[]{:T(128)}, f32[4,64]{1,0:T(4,128)}, f32[4,64,64]{2,1,0:T(8,128)S(1)}, bf16[2,4,64,64]{3,2,1,0:T(8,128)(2,1)S(1)}, bf16[2,4,64,64]{3,2,1,0:T(8...) while((s32[]{:T(128)}, f32[4,64]{1,0:T(4,128)}, ...), condition=%wide.region_22.23_spmd.clone.clone, body=%wide.region_11.22_spmd.clone.clone.sunk | while | flops 556450816 | bytes 38863628 | solution.py:108
  562.1 126.7 %psum.7 = f32[256]{0:T(256)} all-reduce(f32[256]{0:T(256)S(1)} %reshape.495), channel_id=1, replica_groups=mesh['dp'=2,'ctx'=32,'tp'=8] {'dp','ctx'}, use_global_device_ids=true, to_apply=%region_23.24 | all-reduce | flops 256 | bytes 2048 | tf_op jit(solution)/shard_map/psum | solution.py:219
  (1032 shorter events, 481.1 us)
Async XLA Ops:
  33.9 7.0 %collective-permute-start = (f32[4,64,64]{2,1,0:T(8,128)S(1)}, f32[4,64,64]{2,1,0:T(8,128)S(1)}, u32[]{:S(2)}, u32[]{:S(2)}) collective-permute-start(f32[4,64,64]{2,1,0:T(8,128)S(1)} %get-tuple-element.4850), channel_id=1, source_target_pairs={{0,8},{8,16},{16,24},{24,32},{32,40},{40,48},{48,56},{56,64},{64,7... | collective-permute-start | bytes 196616 | tf_op jit(solution)/shard_map/while/body/eval_jaxpr/ppermute | solution.py:13
  38.1 7.5 %collective-permute-start.1 = (f32[4,64,64]{2,1,0:T(8,128)S(1)}, f32[4,64,64]{2,1,0:T(8,128)S(1)}, u32[]{:S(2)}, u32[]{:S(2)}) collective-permute-start(f32[4,64,64]{2,1,0:T(8,128)S(1)} %get-tuple-element.4851), channel_id=1, source_target_pairs={{8,0},{16,8},{24,16},{32,24},{40,32},{48,40},{56,48},{64,56},{72,6... | collective-permute-start | bytes 196616 | tf_op jit(solution)/shard_map/while/body/eval_jaxpr/ppermute | solution.py:13
  50.6 8.4 %collective-permute-start.1 = (f32[4,64,64]{2,1,0:T(8,128)S(1)}, f32[4,64,64]{2,1,0:T(8,128)S(1)}, u32[]{:S(2)}, u32[]{:S(2)}) collective-permute-start(f32[4,64,64]{2,1,0:T(8,128)S(1)} %get-tuple-element.4851), channel_id=1, source_target_pairs={{8,0},{16,8},{24,16},{32,24},{40,32},{48,40},{56,48},{64,56},{72,6... | collective-permute-start | bytes 196616 | tf_op jit(solution)/shard_map/while/body/eval_jaxpr/ppermute | solution.py:13
  59.7 7.4 %collective-permute-start = (f32[4,64,64]{2,1,0:T(8,128)S(1)}, f32[4,64,64]{2,1,0:T(8,128)S(1)}, u32[]{:S(2)}, u32[]{:S(2)}) collective-permute-start(f32[4,64,64]{2,1,0:T(8,128)S(1)} %get-tuple-element.4850), channel_id=1, source_target_pairs={{0,8},{8,16},{16,24},{24,32},{32,40},{40,48},{48,56},{56,64},{64,7... | collective-permute-start | bytes 196616 | tf_op jit(solution)/shard_map/while/body/eval_jaxpr/ppermute | solution.py:13
  64.5 6.9 collective-permute-start.1
  76.0 6.9 collective-permute-start.1
  86.9 6.9 collective-permute-start.1
  97.8 6.9 collective-permute-start.1
  109.2 6.9 collective-permute-start.1
  116.7 7.0 %collective-permute-start = (f32[4,64,64]{2,1,0:T(8,128)S(1)}, f32[4,64,64]{2,1,0:T(8,128)S(1)}, u32[]{:S(2)}, u32[]{:S(2)}) collective-permute-start(f32[4,64,64]{2,1,0:T(8,128)S(1)} %get-tuple-element.4850), channel_id=1, source_target_pairs={{0,8},{8,16},{16,24},{24,32},{32,40},{40,48},{48,56},{56,64},{64,7... | collective-permute-start | bytes 196616 | tf_op jit(solution)/shard_map/while/body/eval_jaxpr/ppermute | solution.py:13
  120.7 7.7 %collective-permute-start.1 = (f32[4,64,64]{2,1,0:T(8,128)S(1)}, f32[4,64,64]{2,1,0:T(8,128)S(1)}, u32[]{:S(2)}, u32[]{:S(2)}) collective-permute-start(f32[4,64,64]{2,1,0:T(8,128)S(1)} %get-tuple-element.4851), channel_id=1, source_target_pairs={{8,0},{16,8},{24,16},{32,24},{40,32},{48,40},{56,48},{64,56},{72,6... | collective-permute-start | bytes 196616 | tf_op jit(solution)/shard_map/while/body/eval_jaxpr/ppermute | solution.py:13
  129.0 7.4 %collective-permute-start = (f32[4,64,64]{2,1,0:T(8,128)S(1)}, f32[4,64,64]{2,1,0:T(8,128)S(1)}, u32[]{:S(2)}, u32[]{:S(2)}) collective-permute-start(f32[4,64,64]{2,1,0:T(8,128)S(1)} %get-tuple-element.4850), channel_id=1, source_target_pairs={{0,8},{8,16},{16,24},{24,32},{32,40},{40,48},{48,56},{56,64},{64,7... | collective-permute-start | bytes 196616 | tf_op jit(solution)/shard_map/while/body/eval_jaxpr/ppermute | solution.py:13
  132.7 8.1 %collective-permute-start.1 = (f32[4,64,64]{2,1,0:T(8,128)S(1)}, f32[4,64,64]{2,1,0:T(8,128)S(1)}, u32[]{:S(2)}, u32[]{:S(2)}) collective-permute-start(f32[4,64,64]{2,1,0:T(8,128)S(1)} %get-tuple-element.4851), channel_id=1, source_target_pairs={{8,0},{16,8},{24,16},{32,24},{40,32},{48,40},{56,48},{64,56},{72,6... | collective-permute-start | bytes 196616 | tf_op jit(solution)/shard_map/while/body/eval_jaxpr/ppermute | solution.py:13
  145.5 6.9 collective-permute-start.1
  157.1 6.9 collective-permute-start.1
  226.4 7.0 %collective-permute-start.1 = (f32[4,64,64]{2,1,0:T(8,128)S(1)}, f32[4,64,64]{2,1,0:T(8,128)S(1)}, u32[]{:S(2)}, u32[]{:S(2)}) collective-permute-start(f32[4,64,64]{2,1,0:T(8,128)S(1)} %get-tuple-element.4851), channel_id=1, source_target_pairs={{8,0},{16,8},{24,16},{32,24},{40,32},{48,40},{56,48},{64,56},{72,6... | collective-permute-start | bytes 196616 | tf_op jit(solution)/shard_map/while/body/eval_jaxpr/ppermute | solution.py:13
  234.0 7.8 %collective-permute-start = (f32[4,64,64]{2,1,0:T(8,128)S(1)}, f32[4,64,64]{2,1,0:T(8,128)S(1)}, u32[]{:S(2)}, u32[]{:S(2)}) collective-permute-start(f32[4,64,64]{2,1,0:T(8,128)S(1)} %get-tuple-element.4850), channel_id=1, source_target_pairs={{0,8},{8,16},{16,24},{24,32},{32,40},{40,48},{48,56},{56,64},{64,7... | collective-permute-start | bytes 196616 | tf_op jit(solution)/shard_map/while/body/eval_jaxpr/ppermute | solution.py:13
  238.0 8.4 %collective-permute-start.1 = (f32[4,64,64]{2,1,0:T(8,128)S(1)}, f32[4,64,64]{2,1,0:T(8,128)S(1)}, u32[]{:S(2)}, u32[]{:S(2)}) collective-permute-start(f32[4,64,64]{2,1,0:T(8,128)S(1)} %get-tuple-element.4851), channel_id=1, source_target_pairs={{8,0},{16,8},{24,16},{32,24},{40,32},{48,40},{56,48},{64,56},{72,6... | collective-permute-start | bytes 196616 | tf_op jit(solution)/shard_map/while/body/eval_jaxpr/ppermute | solution.py:13
  247.1 7.0 %collective-permute-start = (f32[4,64,64]{2,1,0:T(8,128)S(1)}, f32[4,64,64]{2,1,0:T(8,128)S(1)}, u32[]{:S(2)}, u32[]{:S(2)}) collective-permute-start(f32[4,64,64]{2,1,0:T(8,128)S(1)} %get-tuple-element.4850), channel_id=1, source_target_pairs={{0,8},{8,16},{16,24},{24,32},{32,40},{40,48},{48,56},{56,64},{64,7... | collective-permute-start | bytes 196616 | tf_op jit(solution)/shard_map/while/body/eval_jaxpr/ppermute | solution.py:13
  251.1 7.1 %collective-permute-start.1 = (f32[4,64,64]{2,1,0:T(8,128)S(1)}, f32[4,64,64]{2,1,0:T(8,128)S(1)}, u32[]{:S(2)}, u32[]{:S(2)}) collective-permute-start(f32[4,64,64]{2,1,0:T(8,128)S(1)} %get-tuple-element.4851), channel_id=1, source_target_pairs={{8,0},{16,8},{24,16},{32,24},{40,32},{48,40},{56,48},{64,56},{72,6... | collective-permute-start | bytes 196616 | tf_op jit(solution)/shard_map/while/body/eval_jaxpr/ppermute | solution.py:13
  339.6 7.2 %collective-permute-start = (f32[4,64,64]{2,1,0:T(8,128)S(1)}, f32[4,64,64]{2,1,0:T(8,128)S(1)}, u32[]{:S(2)}, u32[]{:S(2)}) collective-permute-start(f32[4,64,64]{2,1,0:T(8,128)S(1)} %get-tuple-element.4850), channel_id=1, source_target_pairs={{0,8},{8,16},{16,24},{24,32},{32,40},{40,48},{48,56},{56,64},{64,7... | collective-permute-start | bytes 196616 | tf_op jit(solution)/shard_map/while/body/eval_jaxpr/ppermute | solution.py:13
  343.6 7.9 %collective-permute-start.1 = (f32[4,64,64]{2,1,0:T(8,128)S(1)}, f32[4,64,64]{2,1,0:T(8,128)S(1)}, u32[]{:S(2)}, u32[]{:S(2)}) collective-permute-start(f32[4,64,64]{2,1,0:T(8,128)S(1)} %get-tuple-element.4851), channel_id=1, source_target_pairs={{8,0},{16,8},{24,16},{32,24},{40,32},{48,40},{56,48},{64,56},{72,6... | collective-permute-start | bytes 196616 | tf_op jit(solution)/shard_map/while/body/eval_jaxpr/ppermute | solution.py:13
  352.2 7.1 %collective-permute-start = (f32[4,64,64]{2,1,0:T(8,128)S(1)}, f32[4,64,64]{2,1,0:T(8,128)S(1)}, u32[]{:S(2)}, u32[]{:S(2)}) collective-permute-start(f32[4,64,64]{2,1,0:T(8,128)S(1)} %get-tuple-element.4850), channel_id=1, source_target_pairs={{0,8},{8,16},{16,24},{24,32},{32,40},{40,48},{48,56},{56,64},{64,7... | collective-permute-start | bytes 196616 | tf_op jit(solution)/shard_map/while/body/eval_jaxpr/ppermute | solution.py:13
  355.9 7.8 %collective-permute-start.1 = (f32[4,64,64]{2,1,0:T(8,128)S(1)}, f32[4,64,64]{2,1,0:T(8,128)S(1)}, u32[]{:S(2)}, u32[]{:S(2)}) collective-permute-start(f32[4,64,64]{2,1,0:T(8,128)S(1)} %get-tuple-element.4851), channel_id=1, source_target_pairs={{8,0},{16,8},{24,16},{32,24},{40,32},{48,40},{56,48},{64,56},{72,6... | collective-permute-start | bytes 196616 | tf_op jit(solution)/shard_map/while/body/eval_jaxpr/ppermute | solution.py:13
  (305 other events, 545.1 us)
where the time goes:
time: 693 us; the launch traced here: 689 us
  starting transfers between devices  164 us (24%)
  waiting for transfers between devices  160 us (23%)
  blocking collectives  127 us (18%)
  local copies, waits for them, and re-layouts  119 us (17%)
  matrix products  98.2 us (14%)
  other arithmetic  16.1 us (2%)
    ppermute x62, starting transfers between devices, passed_along(): return lax.ppermute(value, axis, pairs)  164 us
    ppermute x62, waiting for transfers between devices, passed_along(): return lax.ppermute(value, axis, pairs)  160 us
    psum x1, blocking collectives, local(): extra_summed = lax.psum(derivative_outcomes[6], ('dp', 'ctx'))  127 us
    dot_general x240, matrix products, matmul_hp(): return jnp.einsum(form, left, right, precision=lax.Precision.HIGHEST)  98.2 us
    while x502, local copies, waits for them, and re-layouts  77.3 us
    another operation x43, local copies, waits for them, and re-layouts  24.8 us
  transfers between devices with their start and end apart: 62, of which 62 were waited for; matrix products, arithmetic and copies ran while one was open for 1% of the time, Pallas kernels for 0%

commit v1 on v0

v1 whole, which is shorter than its diff:
```python
import functools

import jax
import jax.numpy as jnp
from jax import lax
from jax.experimental import pallas as pl
from jax.experimental.pallas import tpu as pltpu
from jax.sharding import PartitionSpec as P

HEAD = 64
PAIR = 128
F32 = jnp.float32
BF16 = jnp.bfloat16
MESH = pl.DeviceIdType.MESH
NN = (((1,), (0,)), ((), ()))
NT = (((1,), (1,)), ((), ()))


def split(x):
    high = x.astype(BF16)
    low = (x - high.astype(F32)).astype(BF16)
    return high, low


def mm(x, y, dims=NN):
    return lax.dot_general(x, y, dims, preferred_element_type=F32)


def cat(parts, axis):
    return jnp.concatenate(parts, axis=axis)


def dot3(x, y, dims=NN):
    xh, xl = split(x) if not isinstance(x, tuple) else x
    yh, yl = split(y) if not isinstance(y, tuple) else y
    axis = 0 if dims is NN else 1
    if yh.shape == (PAIR, PAIR):
        wide = cat([cat([yh, yl], 1 - axis)] * 2, axis)
        both = mm(cat([xh, xl], 1), wide, dims)
        return both[:, :PAIR] + both[:, PAIR:]
    return mm(cat([xh, xl], 1), cat([yh, yh], axis), dims) + mm(xh, yl, dims)


def dot2(x, y, dims=NN):
    xh, xl = split(x) if not isinstance(x, tuple) else x
    axis = 0 if dims is NN else 1
    return mm(cat([xh, xl], 1), cat([y, y], axis), dims)


def iotas(rows, cols):
    return (
        lax.broadcasted_iota(jnp.int32, (rows, cols), 0),
        lax.broadcasted_iota(jnp.int32, (rows, cols), 1),
    )


def first_half(shape):
    return (lax.broadcasted_iota(jnp.int32, shape, 1) & (PAIR - 1)) < HEAD


def by_head(stacked):
    half = stacked.shape[0] // 2
    top, bottom = stacked[:half], stacked[half:]
    return jnp.where(first_half(top.shape), top, bottom)


def own_lanes(x):
    mine = first_half(x.shape)
    return jnp.where(mine, x, 0.0), jnp.where(mine, 0.0, x)


def compact(blocks):
    return by_head(blocks)


def spread(x):
    return cat(list(own_lanes(x)), 0)


def turned_lanes(x):
    return pltpu.roll(x, HEAD, 1)


def gram_parts(x):
    high = x.astype(BF16).astype(F32)
    low = x - high
    high_t, low_t = turned_lanes(high), turned_lanes(low)
    mine = first_half(x.shape)
    pick = lambda a, b: jnp.where(mine, a, b).astype(BF16)
    return (
        (pick(high, low_t), pick(high, high_t), pick(low, low_t)),
        (pick(high_t, low), pick(high_t, high), pick(low_t, low)),
    )


def gram(lefts, rights):
    out = []
    for h in (0, 1):
        left = cat([x[h][0] for x in lefts], 0)
        right = [cat([x[h][i] for x in rights], 0) for i in (1, 2)]
        out.append(mm(cat([left, left], 1), cat(right, 1), NT))
    return out


def flip(x):
    return jnp.swapaxes(x, 0, 1)


def prepare(r, k, w, kappa, eta):
    n = w.shape[0]
    row, col = iotas(n, n)
    tri = jnp.where(row >= col, 1.0, 0.0).astype(BF16)
    wh = w.astype(BF16)
    rest = w - wh.astype(F32)
    wm = rest.astype(BF16)
    wl = (rest - wm.astype(F32)).astype(BF16)
    c = mm(cat([tri, tri], 1), cat([wh, wm], 0)) + mm(tri, wl)
    mid = c[n // 2 : n // 2 + 1]
    end = c[n - 1 : n]
    grow = jnp.exp(c - mid)
    fall = jnp.exp(mid - c)
    fall_before = jnp.exp(mid - (c - w))
    beta = kappa * eta
    out = dict(
        end=end,
        grow=grow,
        fall=fall,
        fall_before=fall_before,
        to_start=jnp.exp(-mid),
        to_end=jnp.exp(mid - end),
        beta=beta,
        rs=r * fall,
        ks=k * grow,
        bs=beta * grow,
        asc=-kappa * fall_before,
    )
    out["a0"] = out["asc"] * out["to_start"]
    out["r0"] = out["rs"] * out["to_start"]
    out["bf"] = out["bs"] * out["to_end"]
    out["kf"] = out["ks"] * out["to_end"]
    return out


def inverse(lows):
    n = lows[0].shape[0]
    row, col = iotas(n, n)
    eye = jnp.where(row == col, 1.0, 0.0)
    start = (row >> 4) == (col >> 4)
    d1 = [jnp.where(start, low, 0.0) for low in lows]
    s1 = [split(d) for d in d1]
    d2 = [dot3(s, s) for s in s1]
    s2 = [split(d) for d in d2]
    d4 = [dot3(s, s) for s in s2]
    p4 = [eye + a + b + dot3(s, t) for a, b, s, t in zip(d1, d2, s1, s2)]
    s4 = [split(d) for d in d4]
    d8 = [dot3(s, s) for s in s4]
    p8 = [p + dot3(p, s) for p, s in zip(p4, s4)]
    t = [split(p + dot3(p, d)) for p, d in zip(p8, d8)]
    rest = [jnp.where(start, 0.0, low) for low in lows]
    x1 = [split(dot3(s, r)) for s, r in zip(t, rest)]
    x2 = [split(dot3(s, s)) for s in x1]
    y1 = [a[0].astype(F32) + a[1].astype(F32) + dot3(s, a) for s, a in zip(x1, t)]
    x4 = [split(dot3(s, s)) for s in x2]
    y2 = [y + dot3(s, y) for s, y in zip(x2, y1)]
    return [y + dot3(s, y) for s, y in zip(x4, y2)]


def local_grams(r, k, v, w, kappa, eta, dy, bonus):
    n = w.shape[0]
    q = prepare(r, k, w, kappa, eta)
    q.update(r=r, k=k, v=v, dy=dy, bonus=bonus, vb=v.astype(BF16), dyb=dy.astype(BF16))
    row, col = iotas(n, n)
    pa, pr, pb, pk = [gram_parts(q[name]) for name in ("asc", "rs", "bs", "ks")]
    lower = gram([pa], [pb, pk])
    upper = gram([pb, pk], [pr, pa])
    q["lw"] = [jnp.where(row > col, t[:, :n], 0.0) for t in lower]
    q["lk"] = cat([jnp.where(row > col, t[:, n:], 0.0) for t in lower], 0)
    q["wwt"] = cat([jnp.where(col >= row, t[:n, :n], 0.0) for t in upper], 0)
    q["wkt"] = cat([jnp.where(col >= row, t[n:, :n], 0.0) for t in upper], 0)
    q["lkt"] = cat([jnp.where(col > row, t[n:, n:], 0.0) for t in upper], 0)
    q["z"] = by_head(dot2(q["lk"], q["vb"]))
    q["zd"] = by_head(dot2(q["wwt"], q["dyb"]))
    return q


def local_message(q, t):
    n = q["z"].shape[0]
    eu = by_head(dot3(cat(t, 0), cat([q["a0"], q["z"]], 1)))
    fp = by_head(dot3(cat([flip(x) for x in t], 0), cat([q["bf"], q["zd"]], 1)))
    ml = dot3(flip(q["bf"]), eu)
    row, col = iotas(HEAD, PAIR)
    decay = jnp.where(row == (col & (HEAD - 1)), jnp.exp(-q["end"]), 0.0)
    mt = decay + compact(ml[:, :n])
    lt = compact(ml[:, n:] + dot2(flip(q["kf"]), q["vb"]))
    ht = compact(flip(dot3(flip(q["a0"]), fp[:, n:]) + dot2(flip(q["r0"]), q["dyb"])))
    row, col = iotas(PAIR, PAIR)
    ones = jnp.where((row >> 6) == (col >> 6), 1.0, 0.0).astype(BF16)
    dyv = dot2(q["dy"] * q["v"], ones)
    bonus_part = jnp.sum(dyv * q["r"] * q["k"], axis=0, keepdims=True)
    q.update(eu=eu, fp=fp, ones=ones, dyv=dyv)
    return lt, mt, ht, bonus_part


def exact_parts(x):
    other = turned_lanes(x)
    mine = first_half(x.shape)
    pick = lambda a, b: jnp.where(mine, a, b).astype(BF16)
    return pick(x, 0.0), pick(x, other), pick(other, 0.0), pick(other, x)


def local_rest(q):
    n = q["z"].shape[0]
    eu, fp = q["eu"], q["fp"]
    more = by_head(dot3(q["lkt"], fp))
    kg = q["kf"] + more[:, :n]
    dv = more[:, n:] + by_head(dot2(q["wkt"], q["dyb"]))
    dv = dv + dot2(q["r"] * q["k"] * q["bonus"], q["ones"]) * q["dy"]
    narrow = [*split(eu[:, :n]), *split(fp[:, :n]), *split(kg)]
    narrow += [*exact_parts(q["v"]), *exact_parts(q["dy"])]
    deep = [*split(cat([q["bs"], q["ks"]], 0)), *split(cat([q["rs"], q["asc"]], 0))]
    wide = [eu[:, n:], fp[:, n:], dv, q["dyv"], q["fall"], q["fall_before"], q["grow"]]
    lines = [q["bonus"], q["to_start"], q["to_end"], jnp.exp(-q["end"])]
    return narrow, deep, wide, lines


def final_part(r, k, v, kappa, eta, dy, narrow, deep, wide, lines, st, g):
    n = r.shape[0]
    eh, el, fh, fl, kgh, kgl, *exact = narrow
    by, ry = deep[:2], deep[2:]
    u_own, p_own, dv_own, dyv, fall, fall_before, grow = wide
    bonus, to_start, to_end, decay = lines
    vb, dyb = v.astype(BF16), dy.astype(BF16)
    sb = split(spread(st))
    gb = split(spread(g))
    u = u_own + dot3((eh, el), sb)
    p = p_own + dot3((fh, fl), gb, NT)
    dv = dv_own + dot3((kgh, kgl), gb, NT)
    zero = jnp.zeros((n, PAIR), BF16)
    gv = ((exact[0], exact[1], zero), (exact[2], exact[3], zero))
    gy = ((exact[4], exact[5], zero), (exact[6], exact[7], zero))
    gu, gp = gram_parts(u), gram_parts(p)
    row, col = iotas(2 * n, 2 * n)
    t, s = row & (n - 1), col & (n - 1)
    fwd_mask = t >= s + jnp.where(row >= n, 1, 0)
    bwd_mask = s >= t + jnp.where(col >= n, 1, 0)
    fwd = cat([jnp.where(fwd_mask, m, 0.0) for m in gram([gy, gp], [gu, gv])], 0)
    bwd = cat([jnp.where(bwd_mask, m, 0.0) for m in gram([gu, gv], [gy, gp])], 0)

    def apply(mat, y):
        mh, ml = split(mat)
        both = mm(mh, cat(y, 1))
        return by_head(both[:, :PAIR] + both[:, PAIR:] + mm(ml, y[0]))

    ra = apply(fwd, by)
    bk = apply(bwd, ry)
    uh, ul = split(u)
    ph, pl_ = split(p)
    start = dot3((cat([dyb, ph], 0), cat([zero, pl_], 0)), sb, NT)
    behind = dot3((cat([uh, vb], 0), cat([ul, zero], 0)), gb)
    dr = (ra[:n] + start[:n] * to_start) * fall
    da = (ra[n:] + start[n:] * to_start) * fall_before
    reach = grow * to_end
    final_u = behind[:n] * reach
    final_v = behind[n:] * reach
    db = bk[:n] * grow + final_u
    dk = bk[n:] * grow + final_v
    beta = kappa * eta
    inner = beta * final_u + k * final_v
    through = r * dr - k * dk - beta * db
    behind_a = -kappa * da
    row, col = iotas(n, n)
    from_here = jnp.where(col >= row, 1.0, 0.0).astype(BF16)
    after = jnp.where(col > row, 1.0, 0.0).astype(BF16)
    tail = mm(cat([from_here, from_here], 1), cat(split(through), 0)) + mm(
        cat([after, after], 1), cat(split(behind_a), 0)
    )
    turned = compact(flip(spread(st)))
    anchor = jnp.sum(turned * g, axis=0, keepdims=True) * decay + jnp.sum(
        inner, axis=0, keepdims=True
    )
    return (
        dr + bonus * k * dyv,
        dk + bonus * r * dyv,
        dv,
        -(tail + anchor),
        eta * db - da,
        kappa * db,
    )


def read_tokens(refs, p):
    lanes = slice(PAIR * p, PAIR * p + PAIR)
    return [ref[:, lanes].astype(F32) for ref in refs]


def final_kernel(*refs):
    ins, (state, narrow, deep, wide, done), outs = refs[:6], refs[6:11], refs[11:]
    got = final_part(
        *read_tokens(ins, 1),
        [narrow[i] for i in range(NARROW)],
        [deep[i] for i in range(DEEP)],
        [wide[i] for i in range(WIDE)],
        [state[i : i + 1] for i in range(LINES)],
        state[8:72],
        state[72:136],
    )
    for i, (ref, value) in enumerate(zip(outs, got)):
        ref[:, 0:PAIR] = done[i]
        ref[:, PAIR : 2 * PAIR] = value.astype(ref.dtype)
    for p in (0, 1):
        outs[6][:, PAIR * p : PAIR * p + PAIR] = state[136 + 8 * p : 137 + 8 * p]


ROW = 8
ROWS = 4
SEND = 192
BACK = 128
NARROW, DEEP, WIDE, LINES = 14, 4, 7, 4


def owner_of(p, d):
    return 4 * p + 2 * d


def adder_of(p, d):
    return owner_of(p, d) + 1


def joined(a, b):
    both = dot3(cat([b[1], b[2]], 0), cat([spread(a[1]), spread(a[0])], 1))
    return both[:HEAD, PAIR:] + b[0], both[:HEAD, :PAIR], both[HEAD:, :PAIR] + a[2]


def joined_states(a, b):
    both = dot3(b[1], cat([spread(a[1]), spread(a[0])], 1))
    return both[:, PAIR:] + b[0], both[:, :PAIR], None


def joined_adjoints(a, b):
    both = dot3(cat([b[1], b[2]], 0), spread(a[1]))
    return None, both[:HEAD], both[HEAD:] + a[2]


def copy_to(src, dst, ssem, rsem, where):
    return pltpu.make_async_remote_copy(
        src_ref=src,
        dst_ref=dst,
        send_sem=ssem,
        recv_sem=rsem,
        device_id=where,
        device_id_type=MESH,
    )


def front_kernel(*refs):
    (ins, outs, staged, scratch, sems) = refs[:8], refs[8:13], refs[13:21], refs[21:37], refs[37:]
    state, done = outs[0], outs[4]
    kept = scratch[12:], (*outs[1:4], state)
    scratch = scratch[:12]
    msg, recv, two, tot, xin, back, run, land, term, terms, sums, total = scratch
    in_sem, send_sem, recv_sem, xsend, xsem, osend, osem = sems[:7]
    tsend, tsem, ssend, ssem, gsend, gsem = sems[7:]
    d = lax.axis_index("dp")
    ctx = lax.axis_index("ctx")
    x = ctx // ROW
    z = ctx % ROW
    mine = [z == owner_of(p, d) for p in (0, 1)]
    is_owner = jnp.logical_or(*mine)
    pown = jnp.where(mine[1], 1, 0)
    adds = [z == adder_of(p, d) for p in (0, 1)]
    is_adder = jnp.logical_or(*adds)
    padd = jnp.where(adds[1], 1, 0)

    def at(xx, zz, dd=None):
        place = {"ctx": xx * ROW + zz}
        if dd is not None:
            place["dp"] = dd
        return place

    loads = [
        pltpu.make_async_copy(src, dst, in_sem.at[i])
        for i, (src, dst) in enumerate(zip(ins, staged))
    ]
    for load in loads:
        load.start()

    barrier = pltpu.get_barrier_semaphore()

    def greet(where):
        pl.semaphore_signal(barrier, inc=1, device_id=where, device_id_type=MESH)

    for p in (0, 1):
        for place in (owner_of(p, d), adder_of(p, d)):
            pl.when(z != place)(lambda place=place: greet(at(x, place)))

    @pl.when(is_owner | is_adder)
    def _():
        for j in (2, 3, 6, 7):
            greet(at(x, (2 * d + j) % ROW))

    @pl.when(is_owner)
    def _():
        for j in range(1, ROWS):
            greet(at((x + j) % ROWS, z))

    @pl.when(is_adder)
    def _():
        for j in range(1, ROWS):
            greet(at((x + j) % ROWS, z))
        for j in range(ROWS):
            greet(at((x + j) % ROWS, adder_of(padd, 1 - d), 1 - d))

    for load in loads:
        load.wait()
    def to_owner(p):
        return copy_to(
            msg.at[p], recv.at[z], send_sem.at[p], recv_sem.at[z], at(x, owner_of(p, d))
        )

    parts = []
    for p in (0, 1):
        tokens = read_tokens(staged[:6] + staged[7:], p)
        part = local_grams(*tokens, staged[6][:, PAIR * p : PAIR * p + PAIR])
        low, mid, high, bonus = local_message(part, inverse(part["lw"]))
        parts.append(part)
        msg[p, 0:64] = low
        msg[p, 64:128] = mid
        msg[p, 128:192] = high
        term[p] = jnp.broadcast_to(bonus, (8, PAIR))
        if p == 0:
            pl.when(is_owner)(lambda: pl.semaphore_wait(barrier, ROW - 1 + ROWS - 1))
            pl.when(is_adder)(lambda: pl.semaphore_wait(barrier, ROW - 1 + 2 * ROWS - 1))
            pl.when(jnp.logical_not(is_owner | is_adder))(lambda: pl.semaphore_wait(barrier, 4))
        pl.when(jnp.logical_not(mine[p]))(lambda p=p: to_owner(p).start())

    def to_adder(p):
        return copy_to(
            term.at[p], terms.at[z], tsend.at[p], tsem.at[z], at(x, adder_of(p, d))
        )

    for p in (0, 1):
        pl.when(jnp.logical_not(adds[p]))(lambda p=p: to_adder(p).start())

    for p in (0, 1):
        for ref, values in zip(kept[p], local_rest(parts[p])):
            for i, value in enumerate(values):
                if value.shape[0] == 1:
                    ref[i : i + 1] = value
                else:
                    ref[i] = value

    @pl.when(is_adder)
    def _():
        terms[z] = term[padd]
        for j in range(1, ROW):
            zz = (z + j) % ROW
            copy_to(term.at[0], terms.at[zz], tsend.at[0], tsem.at[zz], at(x, zz)).wait_recv()
        part = terms[0]
        for i in range(1, ROW):
            part = part + terms[i]
        me = d * ROWS + x
        sums[me] = part
        places = [((x + j) % ROWS, d) for j in range(1, ROWS)]
        places += [((x + j) % ROWS, 1 - d) for j in range(ROWS)]
        across = [
            copy_to(
                sums.at[me], sums.at[me], ssend.at[i], ssem.at[me], at(xx, adder_of(padd, dd), dd)
            )
            for i, (xx, dd) in enumerate(places)
        ]
        for copy in across:
            copy.start()
        for xx, dd in places:
            slot = dd * ROWS + xx
            copy_to(
                sums.at[slot], sums.at[slot], ssend.at[0], ssem.at[slot], at(xx, z)
            ).wait_recv()
        part = sums[0]
        for i in range(1, 2 * ROWS):
            part = part + sums[i]
        total[padd] = part
        gives = [
            copy_to(total.at[padd], total.at[padd], gsend.at[j], gsem.at[padd], at(x, (z + j) % ROW))
            for j in range(1, ROW)
        ]
        for give in gives:
            give.start()
        for copy in across + gives:
            copy.wait_send()

    @pl.when(is_owner)
    def _():
        recv[z] = msg[pown]
        for steps in ((0, 1, 3), (2,)):
            places = [(z // 2 + j) % (ROW // 2) for j in steps]
            for j, i in zip(steps, places):
                for zz in (2 * i, 2 * i + 1)[1 if j == 0 else 0 :]:
                    copy_to(
                        msg.at[0], recv.at[zz], send_sem.at[0], recv_sem.at[zz], at(x, zz)
                    ).wait_recv()
            blocks = [
                [(recv[zz, 0:64], recv[zz, 64:128], recv[zz, 128:192]) for zz in (2 * i, 2 * i + 1)]
                for i in places
            ]
            for i, got in zip(places, [joined(*both) for both in blocks]):
                two[i, 0:64] = got[0]
                two[i, 64:128] = got[1]
                two[i, 128:192] = got[2]
        pair = [(two[i, 0:64], two[i, 64:128], two[i, 128:192]) for i in range(ROW // 2)]
        four = [joined(pair[0], pair[1]), joined(pair[2], pair[3])]
        whole = joined(four[0], four[1])
        tot[0:64] = whole[0]
        tot[64:128] = whole[1]
        tot[128:192] = whole[2]
        cases = (
            (lambda xx: (xx > x) & (x == 0), 0, 64),
            (lambda xx: (xx > x) & (x != 0), 0, 128),
            (lambda xx: (xx < x) & (x == ROWS - 1), 128, 192),
            (lambda xx: (xx < x) & (x != ROWS - 1), 64, 192),
        )

        def across(xx, low, high, landing):
            rows = pl.ds(low, high - low)
            return copy_to(
                tot.at[rows], xin.at[landing, rows], xsend.at[xx], xsem.at[landing], at(xx, z)
            )

        for xx in range(ROWS):
            for when, low, high in cases:
                pl.when(when(xx))(
                    lambda xx=xx, low=low, high=high: across(xx, low, high, x).start()
                )
        one = [(recv[i, 0:64], recv[i, 64:128], recv[i, 128:192]) for i in range(ROW)]
        before = [None, one[0], pair[0], None, four[0], None, None, None]
        before[3] = joined_states(pair[0], one[2])
        before[5] = joined_states(four[0], one[4])
        before[6] = joined_states(four[0], pair[2])
        before[7] = joined_states(before[6], one[6])
        behind = [None, None, None, four[1], None, pair[3], one[7], None]
        behind[4] = joined_adjoints(one[5], pair[3])
        behind[2] = joined_adjoints(one[3], four[1])
        behind[1] = joined_adjoints(pair[1], four[1])
        behind[0] = joined_adjoints(one[1], behind[1])

        run[...] = jnp.zeros_like(run)
        for xx in range(ROWS - 1):
            high = 64 if xx == 0 else 128

            @pl.when(x > xx)
            def _(xx=xx, high=high):
                across(xx, 0, high, xx).wait_recv()
                if xx == 0:
                    run[0] = xin[0, 0:64]
                else:
                    run[0] = dot3(xin[xx, 64:128], spread(run[0])) + xin[xx, 0:64]

        for xx in range(ROWS - 1, 0, -1):
            low = 128 if xx == ROWS - 1 else 64

            @pl.when(x < xx)
            def _(xx=xx, low=low):
                across(xx, low, 192, xx).wait_recv()
                if xx == ROWS - 1:
                    run[1] = xin[xx, 128:192]
                else:
                    run[1] = dot3(run[1], spread(xin[xx, 64:128])) + xin[xx, 128:192]

        sg, gg = run[0], run[1]
        moved = dot3(cat([before[i][1] for i in range(1, ROW)], 0), spread(sg))
        for i in range(ROW):
            back[i, 0:64] = sg if i == 0 else moved[64 * i - 64 : 64 * i] + before[i][0]
        gs = split(gg)
        for i in range(0, ROW, 2):
            if i + 1 < ROW - 1:
                got = dot3(gs, cat([spread(behind[i][1]), spread(behind[i + 1][1])], 1))
                back[i, 64:128] = got[:, :PAIR] + behind[i][2]
                back[i + 1, 64:128] = got[:, PAIR:] + behind[i + 1][2]
            else:
                back[i, 64:128] = dot3(gs, spread(behind[i][1])) + behind[i][2]
                back[i + 1, 64:128] = gg

        gives = []
        for j in (4, 3, 5, 2, 6, 1, 7):
            zz = (z + j) % ROW
            gives.append(
                copy_to(back.at[zz], land.at[pown], osend.at[j], osem.at[pown], at(x, zz))
            )
            gives[-1].start()
        land[pown] = back[z]
        for give in gives:
            give.wait_send()
        for xx in range(ROWS):
            for when, low, high in cases:
                pl.when(when(xx))(
                    lambda xx=xx, low=low, high=high: across(xx, low, high, x).wait_send()
                )

    def state_arrives(p):
        @pl.when(jnp.logical_not(mine[p]))
        def _():
            to_owner(p).wait_send()
            copy_to(
                back.at[0], land.at[p], osend.at[0], osem.at[p], at(x, owner_of(p, d))
            ).wait_recv()

    state_arrives(0)
    held, deep_held, wide_held, lines_held = kept[0]
    got = final_part(
        *read_tokens([staged[i] for i in (0, 1, 2, 4, 5, 7)], 0),
        [held[i] for i in range(NARROW)],
        [deep_held[i] for i in range(DEEP)],
        [wide_held[i] for i in range(WIDE)],
        [lines_held[i : i + 1] for i in range(LINES)],
        land[0, 0:64],
        land[0, 64:128],
    )
    for i, value in enumerate(got):
        done[i] = value.astype(done.dtype)
    state_arrives(1)
    state[8:136] = land[1]

    for p in (0, 1):

        @pl.when(jnp.logical_not(adds[p]))
        def _(p=p):
            to_adder(p).wait_send()
            copy_to(
                total.at[p], total.at[p], gsend.at[0], gsem.at[p], at(x, adder_of(p, d))
            ).wait_recv()

    state[136:144] = total[0]
    state[144:152] = total[1]


VMEM = pl.BlockSpec(memory_space=pltpu.VMEM)
HBM = pl.BlockSpec(memory_space=pltpu.HBM)


def local(r, k, v, w, kappa, eta, extra, dy):
    rows, width = r.shape[1], r.shape[2]
    pairs = width // PAIR
    flat = [t.reshape(rows, width) for t in (r, k, v, w, kappa, eta)]
    ins = (*flat, extra.reshape(1, width), dy.reshape(rows, width))
    f32 = lambda *shape: jax.ShapeDtypeStruct(shape, F32)
    dma = lambda n: pltpu.SemaphoreType.DMA((n,))
    bf16 = lambda *shape: jax.ShapeDtypeStruct(shape, BF16)
    kept = pl.pallas_call(
        front_kernel,
        out_shape=(
            f32(BACK + 24, PAIR),
            bf16(NARROW, rows, PAIR),
            bf16(DEEP, 2 * rows, PAIR),
            f32(WIDE, rows, PAIR),
            bf16(6, rows, PAIR),
        ),
        in_specs=[HBM] * 8,
        out_specs=[VMEM] * 5,
        scratch_shapes=[
            *[pltpu.VMEM(t.shape, t.dtype) for t in ins],
            pltpu.VMEM((pairs, SEND, PAIR), F32),
            pltpu.VMEM((ROW, SEND, PAIR), F32),
            pltpu.VMEM((ROW // 2, SEND, PAIR), F32),
            pltpu.VMEM((SEND, PAIR), F32),
            pltpu.VMEM((ROWS, SEND, PAIR), F32),
            pltpu.VMEM((ROW, BACK, PAIR), F32),
            pltpu.VMEM((2, HEAD, PAIR), F32),
            pltpu.VMEM((pairs, BACK, PAIR), F32),
            pltpu.VMEM((pairs, 8, PAIR), F32),
            pltpu.VMEM((ROW, 8, PAIR), F32),
            pltpu.VMEM((2 * ROWS, 8, PAIR), F32),
            pltpu.VMEM((pairs, 8, PAIR), F32),
            pltpu.VMEM((NARROW, rows, PAIR), BF16),
            pltpu.VMEM((DEEP, 2 * rows, PAIR), BF16),
            pltpu.VMEM((WIDE, rows, PAIR), F32),
            pltpu.VMEM((8, PAIR), F32),
            *[dma(n) for n in (8, 2, ROW, ROWS, ROWS, ROW, 2)],
            *[dma(n) for n in (2, ROW, 2 * ROWS, 2 * ROWS, ROW, 2)],
        ],
        compiler_params=pltpu.CompilerParams(
            collective_id=0, has_side_effects=True, vmem_limit_bytes=48 * 1024 * 1024
        ),
    )(*[pltpu.with_memory_space_constraint(t, pltpu.HBM) for t in ins])
    *grads, bonus = pl.pallas_call(
        final_kernel,
        out_shape=(*[bf16(rows, width)] * 6, f32(1, width)),
        in_specs=[VMEM] * 11,
        out_specs=[VMEM] * 7,
        compiler_params=pltpu.CompilerParams(vmem_limit_bytes=40 * 1024 * 1024),
    )(*[ins[i] for i in (0, 1, 2, 4, 5, 7)], *kept)
    return (*[t.reshape(1, rows, width) for t in grads], bonus.reshape(width))


def solution(mesh):
    block = P("dp", "ctx", "tp")
    return jax.shard_map(
        local,
        mesh=mesh,
        in_specs=(block,) * 6 + (P("tp"), block),
        out_specs=(block,) * 6 + (P("tp"),),
        check_vma=False,
    )
```

time: 693 us -> 37.9 us (0.05)
  starting transfers between devices: 164 us -> 0 us
  waiting for transfers between devices: 160 us -> 0 us
  blocking collectives: 127 us -> 0 us
  local copies, waits for them, and re-layouts: 119 us -> 0.03 us
  matrix products: 98.2 us -> 0 us
  Pallas kernels: 0 us -> 37 us
  other arithmetic: 16.1 us -> 0 us
    ppermute x62 -> x0, starting transfers between devices: 164 us -> none  [passed_along(): return lax.ppermute(value, axis, pairs)]
    ppermute x62 -> x0, waiting for transfers between devices: 160 us -> none  [passed_along(): return lax.ppermute(value, axis, pairs)]
    psum x1 -> x0, blocking collectives: 127 us -> none  [local(): extra_summed = lax.psum(derivative_outcomes[6], ('dp', 'ctx'))]
    dot_general x240 -> x0, matrix products: 98.2 us -> none  [matmul_hp(): return jnp.einsum(form, left, right, precision=lax.Precision.HIGHEST)]
    while x503 -> x0, local copies, waits for them, and re-layouts: 77.4 us -> none
    pallas_call x0 -> x2, Pallas kernels: none -> 37 us  [the longest x1 35.1 us: local(): pl.pallas_call(front_kernel, out_shape=(f32(BACK + 24, PAIR), bf16(NARROW...]
    another operation x43 -> x0, local copies, waits for them, and re-layouts: 24.8 us -> none
    unnamed x47 -> x12, local copies, waits for them, and re-layouts: 8.98 us -> 0.03 us
  transfers between devices with their start and end apart: 62 -> 0, of which waited for: 62 -> 0; matrix products, arithmetic and copies ran while one was open for 1% -> 0% of each run, Pallas kernels for 0% -> 0%
where the time goes in v1:
time: 37.9 us; the launch traced here: 37.7 us
  Pallas kernels  37 us (98%)
  between operations  0.74 us (2%)
    pallas_call x1, Pallas kernels, local(): pl.pallas_call(front_kernel, out_shape=(f32(BACK + 24, PAIR), bf16(NARROW...  35.1 us
    pallas_call x1, Pallas kernels, local(): pl.pallas_call(final_kernel, out_shape=(*[bf16(rows, width)] * 6, f32(1,...  1.85 us

profile of v1, /device:TPU:56, one launch (start us, length us, event | category | flops | bytes accessed | tf_op | source)
XLA Modules:
  0.0 37.7 jit_solution(15703373131141914512)
XLA Ops:
  0.6 0.0 copy-start
  0.6 0.0 copy-start.1
  0.7 0.0 copy-start.2
  0.7 0.0 copy-start.3
  0.7 0.0 copy-start.4
  0.7 0.0 copy-start.5
  0.7 35.1 %shard_map.135 = (f32[152,128]{1,0:T(8,128)S(1)}, bf16[14,128,128]{2,1,0:T(8,128)(2,1)S(1)}, bf16[4,256,128]{2,1,0:T(8,128)(2,1)S(1)}, f32[7,128,128]{2,1,0:T(8,128)S(1)}, bf16[6,128,128]{2,1,0:T(8,128)(2,1)S(1)}) custom-call(bf16[128,256]{1,0:T(8,128)(2,1)} %bitcast.15, bf16[128,256]{1,0:T(8,128)(2,1)} %bitcast.17, bf16[128,256]{1,0:T(8,128)(2,1)} %bitcast.19, ...), custom_call_target="tpu_custom_call" | custom-call | tf_op jit(solution)/shard_map/pallas_call | solution.py:647
  35.8 0.0 copy-done
  35.8 0.0 copy-done.1
  35.9 0.0 copy-done.2
  35.9 0.0 copy-done.3
  35.9 0.0 copy-done.4
  35.9 0.0 copy-done.5
  35.9 1.9 %shard_map.136 = (bf16[128,256]{1,0:T(8,128)(2,1)}, bf16[128,256]{1,0:T(8,128)(2,1)}, bf16[128,256]{1,0:T(8,128)(2,1)}, bf16[128,256]{1,0:T(8,128)(2,1)}, bf16[1...) custom-call(bf16[128,256]{1,0:T(8,128)(2,1)S(1)} %bitcast.16, bf16[128,256]{1,0:T(8,128)(2,1)S(1)} %bitcast.18, ...), custom_call_target="tpu_custom_call" | custom-call | tf_op jit(solution)/shard_map/pallas_call | solution.py:683
Async XLA Ops:
  0.6 35.2 %copy-start = (bf16[1,128,256]{2,1,0:T(8,128)(2,1)S(1)}, bf16[1,128,256]{2,1,0:T(8,128)(2,1)}, u32[]{:S(2)}) copy-start(bf16[1,128,256]{2,1,0:T(8,128)(2,1)} %param.8) | copy-start | bytes 196612
  0.6 35.2 %copy-start.1 = (bf16[1,128,256]{2,1,0:T(8,128)(2,1)S(1)}, bf16[1,128,256]{2,1,0:T(8,128)(2,1)}, u32[]{:S(2)}) copy-start(bf16[1,128,256]{2,1,0:T(8,128)(2,1)} %param.9) | copy-start | bytes 196612
  0.7 35.2 %copy-start.2 = (bf16[1,128,256]{2,1,0:T(8,128)(2,1)S(1)}, bf16[1,128,256]{2,1,0:T(8,128)(2,1)}, u32[]{:S(2)}) copy-start(bf16[1,128,256]{2,1,0:T(8,128)(2,1)} %param.10) | copy-start | bytes 196612
  0.7 35.2 %copy-start.3 = (bf16[1,128,256]{2,1,0:T(8,128)(2,1)S(1)}, bf16[1,128,256]{2,1,0:T(8,128)(2,1)}, u32[]{:S(2)}) copy-start(bf16[1,128,256]{2,1,0:T(8,128)(2,1)} %param.12) | copy-start | bytes 196612
  0.7 35.2 %copy-start.4 = (bf16[1,128,256]{2,1,0:T(8,128)(2,1)S(1)}, bf16[1,128,256]{2,1,0:T(8,128)(2,1)}, u32[]{:S(2)}) copy-start(bf16[1,128,256]{2,1,0:T(8,128)(2,1)} %param.13) | copy-start | bytes 196612
  0.7 35.2 %copy-start.5 = (bf16[1,128,256]{2,1,0:T(8,128)(2,1)S(1)}, bf16[1,128,256]{2,1,0:T(8,128)(2,1)}, u32[]{:S(2)}) copy-start(bf16[1,128,256]{2,1,0:T(8,128)(2,1)} %param.15) | copy-start | bytes 196612

commit v2 on v1

--- a/solution.py
+++ b/solution.py
@@ -294,21 +294,24 @@
 
 
 def final_kernel(*refs):
-    ins, (state, narrow, deep, wide, done), outs = refs[:6], refs[6:11], refs[11:]
-    got = final_part(
-        *read_tokens(ins, 1),
-        [narrow[i] for i in range(NARROW)],
-        [deep[i] for i in range(DEEP)],
-        [wide[i] for i in range(WIDE)],
-        [state[i : i + 1] for i in range(LINES)],
-        state[8:72],
-        state[72:136],
-    )
-    for i, (ref, value) in enumerate(zip(outs, got)):
-        ref[:, 0:PAIR] = done[i]
-        ref[:, PAIR : 2 * PAIR] = value.astype(ref.dtype)
-    for p in (0, 1):
-        outs[6][:, PAIR * p : PAIR * p + PAIR] = state[136 + 8 * p : 137 + 8 * p]
+    ins, (state, narrow, deep, wide), outs = refs[:6], refs[6:10], refs[10:]
+    got = [
+        final_part(
+            *read_tokens(ins, p),
+            [narrow[p, i] for i in range(NARROW)],
+            [deep[p, i] for i in range(DEEP)],
+            [wide[p, i] for i in range(WIDE)],
+            [state[p, BACK + 8 + i : BACK + 9 + i] for i in range(LINES)],
+            state[p, 0:64],
+            state[p, 64:128],
+        )
+        for p in (0, 1)
+    ]
+    for p in (0, 1):
+        lanes = slice(PAIR * p, PAIR * p + PAIR)
+        for ref, value in zip(outs, got[p]):
+            ref[:, lanes] = value.astype(ref.dtype)
+        outs[6][:, lanes] = state[p, BACK : BACK + 1]
 
 
 ROW = 8
@@ -353,10 +356,8 @@
 
 
 def front_kernel(*refs):
-    (ins, outs, staged, scratch, sems) = refs[:8], refs[8:13], refs[13:21], refs[21:37], refs[37:]
-    state, done = outs[0], outs[4]
-    kept = scratch[12:], (*outs[1:4], state)
-    scratch = scratch[:12]
+    (ins, outs, staged, scratch, sems) = refs[:8], refs[8:12], refs[12:20], refs[20:32], refs[32:]
+    state, narrow, deep, wide = outs
     msg, recv, two, tot, xin, back, run, land, term, terms, sums, total = scratch
     in_sem, send_sem, recv_sem, xsend, xsem, osend, osem = sems[:7]
     tsend, tsem, ssend, ssem, gsend, gsem = sems[7:]
@@ -412,26 +413,55 @@
 
     for load in loads:
         load.wait()
+    parts = []
+    for p in (0, 1):
+        tokens = read_tokens(staged[:6] + staged[7:], p)
+        parts.append(local_grams(*tokens, staged[6][:, PAIR * p : PAIR * p + PAIR]))
+    solved = inverse(parts[0]["lw"] + parts[1]["lw"])
+
     def to_owner(p):
-        return copy_to(
-            msg.at[p], recv.at[z], send_sem.at[p], recv_sem.at[z], at(x, owner_of(p, d))
-        )
-
-    parts = []
-    for p in (0, 1):
-        tokens = read_tokens(staged[:6] + staged[7:], p)
-        part = local_grams(*tokens, staged[6][:, PAIR * p : PAIR * p + PAIR])
-        low, mid, high, bonus = local_message(part, inverse(part["lw"]))
-        parts.append(part)
+        place = jnp.where(is_owner, (z + 1) % ROW, owner_of(p, d))
+        return copy_to(msg.at[p], recv.at[z], send_sem.at[p], recv_sem.at[z], at(x, place))
+
+    pmate = 1 - padd
+
+    def from_mate(p, slot, i, place):
+        return copy_to(tot, two.at[i], send_sem.at[p], recv_sem.at[slot], place)
+
+    messages = [local_message(parts[p], solved[2 * p : 2 * p + 2]) for p in (0, 1)]
+    for p, (low, mid, high, bonus) in enumerate(messages):
         msg[p, 0:64] = low
         msg[p, 64:128] = mid
         msg[p, 128:192] = high
         term[p] = jnp.broadcast_to(bonus, (8, PAIR))
-        if p == 0:
-            pl.when(is_owner)(lambda: pl.semaphore_wait(barrier, ROW - 1 + ROWS - 1))
-            pl.when(is_adder)(lambda: pl.semaphore_wait(barrier, ROW - 1 + 2 * ROWS - 1))
-            pl.when(jnp.logical_not(is_owner | is_adder))(lambda: pl.semaphore_wait(barrier, 4))
-        pl.when(jnp.logical_not(mine[p]))(lambda p=p: to_owner(p).start())
+    pl.when(is_owner)(lambda: pl.semaphore_wait(barrier, ROW - 1 + ROWS - 1))
+    pl.when(is_adder)(lambda: pl.semaphore_wait(barrier, ROW - 1 + 2 * ROWS - 1))
+    pl.when(jnp.logical_not(is_owner | is_adder))(lambda: pl.semaphore_wait(barrier, 4))
+    for p in (0, 1):
+        direct = jnp.logical_not(mine[p] | adds[1 - p])
+        pl.when(direct)(lambda p=p: to_owner(p).start())
+
+    def over_mate(place):
+        rows = pl.ds(64, 128)
+        return copy_to(
+            msg.at[pmate, rows], xin.at[x, rows], xsend.at[0], xsem.at[x], at(x, place)
+        )
+
+    @pl.when(is_adder)
+    def _():
+        far = (z + ROW - 1) % ROW
+        over_mate(far).start()
+        copy_to(
+            msg.at[0], recv.at[far], send_sem.at[0], recv_sem.at[far], at(x, far)
+        ).wait_recv()
+        got = joined(
+            (recv[far, 0:64], recv[far, 64:128], recv[far, 128:192]),
+            (msg[pmate, 0:64], msg[pmate, 64:128], msg[pmate, 128:192]),
+        )
+        tot[0:64] = got[0]
+        tot[64:128] = got[1]
+        tot[128:192] = got[2]
+        from_mate(pmate, z, z // 2, at(x, owner_of(pmate, d))).start()
 
     def to_adder(p):
         return copy_to(
@@ -442,12 +472,12 @@
         pl.when(jnp.logical_not(adds[p]))(lambda p=p: to_adder(p).start())
 
     for p in (0, 1):
-        for ref, values in zip(kept[p], local_rest(parts[p])):
+        got = local_rest(parts[p])
+        for ref, values in zip((narrow, deep, wide), got):
             for i, value in enumerate(values):
-                if value.shape[0] == 1:
-                    ref[i : i + 1] = value
-                else:
-                    ref[i] = value
+                ref[p, i] = value
+        for i, line in enumerate(got[3]):
+            state[p, BACK + 8 + i : BACK + 9 + i] = line
 
     @pl.when(is_adder)
     def _():
@@ -491,21 +521,24 @@
     @pl.when(is_owner)
     def _():
         recv[z] = msg[pown]
-        for steps in ((0, 1, 3), (2,)):
-            places = [(z // 2 + j) % (ROW // 2) for j in steps]
-            for j, i in zip(steps, places):
-                for zz in (2 * i, 2 * i + 1)[1 if j == 0 else 0 :]:
-                    copy_to(
-                        msg.at[0], recv.at[zz], send_sem.at[0], recv_sem.at[zz], at(x, zz)
-                    ).wait_recv()
-            blocks = [
-                [(recv[zz, 0:64], recv[zz, 64:128], recv[zz, 128:192]) for zz in (2 * i, 2 * i + 1)]
-                for i in places
-            ]
-            for i, got in zip(places, [joined(*both) for both in blocks]):
-                two[i, 0:64] = got[0]
-                two[i, 64:128] = got[1]
-                two[i, 128:192] = got[2]
+        far = (z + ROW // 2) % ROW
+        for zz in (far, far + 1):
+            recv[zz] = jnp.zeros((SEND, PAIR), F32)
+        places = [(z // 2 + j) % (ROW // 2) for j in (0, 1, 3)]
+        for j, i in zip((0, 1, 3), places):
+            for zz in (2 * i + 1,) if j == 0 else (2 * i, 2 * i + 1):
+                copy_to(
+                    msg.at[0], recv.at[zz], send_sem.at[0], recv_sem.at[zz], at(x, zz)
+                ).wait_recv()
+        blocks = [
+            [(recv[zz, 0:64], recv[zz, 64:128], recv[zz, 128:192]) for zz in (2 * i, 2 * i + 1)]
+            for i in places
+        ]
+        for i, got in zip(places, [joined(*both) for both in blocks]):
+            two[i, 0:64] = got[0]
+            two[i, 64:128] = got[1]
+            two[i, 128:192] = got[2]
+        from_mate(0, far + 1, far // 2, at(x, far + 1)).wait_recv()
         pair = [(two[i, 0:64], two[i, 64:128], two[i, 128:192]) for i in range(ROW // 2)]
         four = [joined(pair[0], pair[1]), joined(pair[2], pair[3])]
         whole = joined(four[0], four[1])
@@ -579,11 +612,13 @@
                 back[i, 64:128] = dot3(gs, spread(behind[i][1])) + behind[i][2]
                 back[i + 1, 64:128] = gg
 
+        back[far + 1, 0:64] = back[far, 0:64]
         gives = []
-        for j in (4, 3, 5, 2, 6, 1, 7):
+        for j in (4, 5, 3, 2, 6, 1, 7):
             zz = (z + j) % ROW
+            source = back.at[far + 1] if j == 4 else back.at[zz]
             gives.append(
-                copy_to(back.at[zz], land.at[pown], osend.at[j], osem.at[pown], at(x, zz))
+                copy_to(source, land.at[pown], osend.at[j], osem.at[pown], at(x, zz))
             )
             gives[-1].start()
         land[pown] = back[z]
@@ -595,29 +630,25 @@
                     lambda xx=xx, low=low, high=high: across(xx, low, high, x).wait_send()
                 )
 
-    def state_arrives(p):
+    for p in (0, 1):
+
         @pl.when(jnp.logical_not(mine[p]))
-        def _():
+        def _(p=p):
             to_owner(p).wait_send()
             copy_to(
                 back.at[0], land.at[p], osend.at[0], osem.at[p], at(x, owner_of(p, d))
             ).wait_recv()
 
-    state_arrives(0)
-    held, deep_held, wide_held, lines_held = kept[0]
-    got = final_part(
-        *read_tokens([staged[i] for i in (0, 1, 2, 4, 5, 7)], 0),
-        [held[i] for i in range(NARROW)],
-        [deep_held[i] for i in range(DEEP)],
-        [wide_held[i] for i in range(WIDE)],
-        [lines_held[i : i + 1] for i in range(LINES)],
-        land[0, 0:64],
-        land[0, 64:128],
-    )
-    for i, value in enumerate(got):
-        done[i] = value.astype(done.dtype)
-    state_arrives(1)
-    state[8:136] = land[1]
+        @pl.when(adds[1 - p])
+        def _(p=p):
+            far = (z + ROW - 1) % ROW
+            land[p, 0:64] = dot3(recv[far, 64:128], spread(land[p, 0:64])) + recv[far, 0:64]
+
+        @pl.when(mine[1 - p])
+        def _(p=p):
+            over_mate(z).wait_recv()
+            over = dot3(land[p, 64:128], spread(xin[x, 64:128]))
+            land[p, 64:128] = over + xin[x, 128:192]
 
     for p in (0, 1):
 
@@ -628,8 +659,13 @@
                 total.at[p], total.at[p], gsend.at[0], gsem.at[p], at(x, adder_of(p, d))
             ).wait_recv()
 
-    state[136:144] = total[0]
-    state[144:152] = total[1]
+    @pl.when(is_adder)
+    def _():
+        over_mate(z).wait_send()
+
+    for p in (0, 1):
+        state[p, 0:BACK] = land[p]
+        state[p, BACK : BACK + 8] = total[p]
 
 
 VMEM = pl.BlockSpec(memory_space=pltpu.VMEM)
@@ -647,14 +683,13 @@
     kept = pl.pallas_call(
         front_kernel,
         out_shape=(
-            f32(BACK + 24, PAIR),
-            bf16(NARROW, rows, PAIR),
-            bf16(DEEP, 2 * rows, PAIR),
-            f32(WIDE, rows, PAIR),
-            bf16(6, rows, PAIR),
+            f32(pairs, BACK + 16, PAIR),
+            bf16(pairs, NARROW, rows, PAIR),
+            bf16(pairs, DEEP, 2 * rows, PAIR),
+            f32(pairs, WIDE, rows, PAIR),
         ),
         in_specs=[HBM] * 8,
-        out_specs=[VMEM] * 5,
+        out_specs=[VMEM] * 4,
         scratch_shapes=[
             *[pltpu.VMEM(t.shape, t.dtype) for t in ins],
             pltpu.VMEM((pairs, SEND, PAIR), F32),
@@ -669,10 +704,6 @@
             pltpu.VMEM((ROW, 8, PAIR), F32),
             pltpu.VMEM((2 * ROWS, 8, PAIR), F32),
             pltpu.VMEM((pairs, 8, PAIR), F32),
-            pltpu.VMEM((NARROW, rows, PAIR), BF16),
-            pltpu.VMEM((DEEP, 2 * rows, PAIR), BF16),
-            pltpu.VMEM((WIDE, rows, PAIR), F32),
-            pltpu.VMEM((8, PAIR), F32),
             *[dma(n) for n in (8, 2, ROW, ROWS, ROWS, ROW, 2)],
             *[dma(n) for n in (2, ROW, 2 * ROWS, 2 * ROWS, ROW, 2)],
         ],
@@ -683,7 +714,7 @@
     *grads, bonus = pl.pallas_call(
         final_kernel,
         out_shape=(*[bf16(rows, width)] * 6, f32(1, width)),
-        in_specs=[VMEM] * 11,
+        in_specs=[VMEM] * 10,
         out_specs=[VMEM] * 7,
         compiler_params=pltpu.CompilerParams(vmem_limit_bytes=40 * 1024 * 1024),
     )(*[ins[i] for i in (0, 1, 2, 4, 5, 7)], *kept)

time: 37.9 us -> 36.1 us (0.953)
  Pallas kernels: 37 us -> 35.1 us
    pallas_call x1, Pallas kernels: 35.1 us -> 32.2 us  [local(): pl.pallas_call(front_kernel, out_shape=(f32(pairs, BACK + 16, PAIR), bf16...]
    pallas_call x1, Pallas kernels: 1.85 us -> 2.85 us  [local(): pl.pallas_call(final_kernel, out_shape=(*[bf16(rows, width)] * 6, f32(1,...]
where the time goes in v2:
time: 36.1 us; the launch traced here: 35.9 us
  Pallas kernels  35.1 us (97%)
  between operations  0.74 us (2%)
    pallas_call x1, Pallas kernels, local(): pl.pallas_call(front_kernel, out_shape=(f32(pairs, BACK + 16, PAIR), bf16...  32.2 us
    pallas_call x1, Pallas kernels, local(): pl.pallas_call(final_kernel, out_shape=(*[bf16(rows, width)] * 6, f32(1,...  2.85 us

profile of v2, /device:TPU:56, one launch (start us, length us, event | category | flops | bytes accessed | tf_op | source)
XLA Modules:
  0.0 35.9 jit_solution(9671009987339946281)
XLA Ops:
  0.6 0.0 copy-start
  0.6 0.0 copy-start.1
  0.7 0.0 copy-start.2
  0.7 0.0 copy-start.3
  0.7 0.0 copy-start.4
  0.7 0.0 copy-start.5
  0.7 32.2 %shard_map.135 = (f32[2,144,128]{2,1,0:T(8,128)S(1)}, bf16[2,14,128,128]{3,2,1,0:T(8,128)(2,1)S(1)}, bf16[2,4,256,128]{3,2,1,0:T(8,128)(2,1)S(1)}, f32[2,7,128,128]{3,2,1,0:T(8,128)S(1)}) custom-call(bf16[128,256]{1,0:T(8,128)(2,1)} %bitcast.15, bf16[128,256]{1,0:T(8,128)(2,1)} %bitcast.17, bf16[128,256]{1,0:T(8,128)(2,1)} %bitcast.19, f32[128,256]{1,0:T(8,128)} %bitcast.27, ...), custom_call_target="tpu_custom_call" | custom-call | tf_op jit(solution)/shard_map/pallas_call | solution.py:683
  32.9 0.0 copy-done
  33.0 0.0 copy-done.1
  33.0 0.0 copy-done.2
  33.0 0.0 copy-done.3
  33.0 0.0 copy-done.4
  33.0 0.0 copy-done.5
  33.0 2.9 %shard_map.136 = (bf16[128,256]{1,0:T(8,128)(2,1)}, bf16[128,256]{1,0:T(8,128)(2,1)}, bf16[128,256]{1,0:T(8,128)(2,1)}, bf16[128,256]{1,0:T(8,128)(2,1)}, bf16[1...) custom-call(bf16[128,256]{1,0:T(8,128)(2,1)S(1)} %bitcast.16, bf16[128,256]{1,0:T(8,128)(2,1)S(1)} %bitcast.18, ...), custom_call_target="tpu_custom_call" | custom-call | tf_op jit(solution)/shard_map/pallas_call | solution.py:714
Async XLA Ops:
  0.6 32.3 %copy-start = (bf16[1,128,256]{2,1,0:T(8,128)(2,1)S(1)}, bf16[1,128,256]{2,1,0:T(8,128)(2,1)}, u32[]{:S(2)}) copy-start(bf16[1,128,256]{2,1,0:T(8,128)(2,1)} %param.8) | copy-start | bytes 196612
  0.6 32.3 %copy-start.1 = (bf16[1,128,256]{2,1,0:T(8,128)(2,1)S(1)}, bf16[1,128,256]{2,1,0:T(8,128)(2,1)}, u32[]{:S(2)}) copy-start(bf16[1,128,256]{2,1,0:T(8,128)(2,1)} %param.9) | copy-start | bytes 196612
  0.7 32.3 %copy-start.2 = (bf16[1,128,256]{2,1,0:T(8,128)(2,1)S(1)}, bf16[1,128,256]{2,1,0:T(8,128)(2,1)}, u32[]{:S(2)}) copy-start(bf16[1,128,256]{2,1,0:T(8,128)(2,1)} %param.10) | copy-start | bytes 196612
  0.7 32.3 %copy-start.3 = (bf16[1,128,256]{2,1,0:T(8,128)(2,1)S(1)}, bf16[1,128,256]{2,1,0:T(8,128)(2,1)}, u32[]{:S(2)}) copy-start(bf16[1,128,256]{2,1,0:T(8,128)(2,1)} %param.12) | copy-start | bytes 196612
  0.7 32.3 %copy-start.4 = (bf16[1,128,256]{2,1,0:T(8,128)(2,1)S(1)}, bf16[1,128,256]{2,1,0:T(8,128)(2,1)}, u32[]{:S(2)}) copy-start(bf16[1,128,256]{2,1,0:T(8,128)(2,1)} %param.13) | copy-start | bytes 196612
  0.7 32.3 %copy-start.5 = (bf16[1,128,256]{2,1,0:T(8,128)(2,1)S(1)}, bf16[1,128,256]{2,1,0:T(8,128)(2,1)}, u32[]{:S(2)}) copy-start(bf16[1,128,256]{2,1,0:T(8,128)(2,1)} %param.15) | copy-start | bytes 196612

commit v3 on v2

--- a/solution.py
+++ b/solution.py
@@ -172,12 +172,11 @@
     row, col = iotas(n, n)
     pa, pr, pb, pk = [gram_parts(q[name]) for name in ("asc", "rs", "bs", "ks")]
     lower = gram([pa], [pb, pk])
-    upper = gram([pb, pk], [pr, pa])
+    upper = gram([pb], [pr])
+    q["late"] = pk, pr, pa
     q["lw"] = [jnp.where(row > col, t[:, :n], 0.0) for t in lower]
     q["lk"] = cat([jnp.where(row > col, t[:, n:], 0.0) for t in lower], 0)
-    q["wwt"] = cat([jnp.where(col >= row, t[:n, :n], 0.0) for t in upper], 0)
-    q["wkt"] = cat([jnp.where(col >= row, t[n:, :n], 0.0) for t in upper], 0)
-    q["lkt"] = cat([jnp.where(col > row, t[n:, n:], 0.0) for t in upper], 0)
+    q["wwt"] = cat([jnp.where(col >= row, t, 0.0) for t in upper], 0)
     q["z"] = by_head(dot2(q["lk"], q["vb"]))
     q["zd"] = by_head(dot2(q["wwt"], q["dyb"]))
     return q
@@ -193,12 +192,16 @@
     mt = decay + compact(ml[:, :n])
     lt = compact(ml[:, n:] + dot2(flip(q["kf"]), q["vb"]))
     ht = compact(flip(dot3(flip(q["a0"]), fp[:, n:]) + dot2(flip(q["r0"]), q["dyb"])))
+    q.update(eu=eu, fp=fp)
+    return lt, mt, ht
+
+
+def bonus_terms(q):
     row, col = iotas(PAIR, PAIR)
     ones = jnp.where((row >> 6) == (col >> 6), 1.0, 0.0).astype(BF16)
     dyv = dot2(q["dy"] * q["v"], ones)
-    bonus_part = jnp.sum(dyv * q["r"] * q["k"], axis=0, keepdims=True)
-    q.update(eu=eu, fp=fp, ones=ones, dyv=dyv)
-    return lt, mt, ht, bonus_part
+    q.update(ones=ones, dyv=dyv)
+    return jnp.sum(dyv * q["r"] * q["k"], axis=0, keepdims=True)
 
 
 def exact_parts(x):
@@ -211,9 +214,14 @@
 def local_rest(q):
     n = q["z"].shape[0]
     eu, fp = q["eu"], q["fp"]
-    more = by_head(dot3(q["lkt"], fp))
+    pk, pr, pa = q["late"]
+    upper = gram([pk], [pr, pa])
+    row, col = iotas(n, n)
+    wkt = cat([jnp.where(col >= row, t[:, :n], 0.0) for t in upper], 0)
+    lkt = cat([jnp.where(col > row, t[:, n:], 0.0) for t in upper], 0)
+    more = by_head(dot3(lkt, fp))
     kg = q["kf"] + more[:, :n]
-    dv = more[:, n:] + by_head(dot2(q["wkt"], q["dyb"]))
+    dv = more[:, n:] + by_head(dot2(wkt, q["dyb"]))
     dv = dv + dot2(q["r"] * q["k"] * q["bonus"], q["ones"]) * q["dy"]
     narrow = [*split(eu[:, :n]), *split(fp[:, :n]), *split(kg)]
     narrow += [*exact_parts(q["v"]), *exact_parts(q["dy"])]
@@ -429,17 +437,19 @@
         return copy_to(tot, two.at[i], send_sem.at[p], recv_sem.at[slot], place)
 
     messages = [local_message(parts[p], solved[2 * p : 2 * p + 2]) for p in (0, 1)]
-    for p, (low, mid, high, bonus) in enumerate(messages):
+    for p, (low, mid, high) in enumerate(messages):
         msg[p, 0:64] = low
         msg[p, 64:128] = mid
         msg[p, 128:192] = high
-        term[p] = jnp.broadcast_to(bonus, (8, PAIR))
     pl.when(is_owner)(lambda: pl.semaphore_wait(barrier, ROW - 1 + ROWS - 1))
     pl.when(is_adder)(lambda: pl.semaphore_wait(barrier, ROW - 1 + 2 * ROWS - 1))
     pl.when(jnp.logical_not(is_owner | is_adder))(lambda: pl.semaphore_wait(barrier, 4))
     for p in (0, 1):
         direct = jnp.logical_not(mine[p] | adds[1 - p])
         pl.when(direct)(lambda p=p: to_owner(p).start())
+
+    for p in (0, 1):
+        term[p] = jnp.broadcast_to(bonus_terms(parts[p]), (8, PAIR))
 
     def over_mate(place):
         rows = pl.ds(64, 128)

time: 36.1 us -> 36.2 us (level)
  no operation moved by 1% of the time
where the time goes in v3:
time: 36.2 us; the launch traced here: 35.9 us
  Pallas kernels  35.1 us (97%)
  between operations  0.74 us (2%)
    pallas_call x1, Pallas kernels, local(): pl.pallas_call(front_kernel, out_shape=(f32(pairs, BACK + 16, PAIR), bf16...  32.3 us
    pallas_call x1, Pallas kernels, local(): pl.pallas_call(final_kernel, out_shape=(*[bf16(rows, width)] * 6, f32(1,...  2.85 us

profile of v3, /device:TPU:56, one launch (start us, length us, event | category | flops | bytes accessed | tf_op | source)
XLA Modules:
  0.0 35.9 jit_solution(956177547638510334)
XLA Ops:
  0.6 0.0 copy-start
  0.6 0.0 copy-start.1
  0.7 0.0 copy-start.2
  0.7 0.0 copy-start.3
  0.7 0.0 copy-start.4
  0.7 0.0 copy-start.5
  0.7 32.3 %shard_map.135 = (f32[2,144,128]{2,1,0:T(8,128)S(1)}, bf16[2,14,128,128]{3,2,1,0:T(8,128)(2,1)S(1)}, bf16[2,4,256,128]{3,2,1,0:T(8,128)(2,1)S(1)}, f32[2,7,128,128]{3,2,1,0:T(8,128)S(1)}) custom-call(bf16[128,256]{1,0:T(8,128)(2,1)} %bitcast.15, bf16[128,256]{1,0:T(8,128)(2,1)} %bitcast.17, bf16[128,256]{1,0:T(8,128)(2,1)} %bitcast.19, f32[128,256]{1,0:T(8,128)} %bitcast.27, ...), custom_call_target="tpu_custom_call" | custom-call | tf_op jit(solution)/shard_map/pallas_call | solution.py:693
  33.0 0.0 copy-done
  33.0 0.0 copy-done.1
  33.0 0.0 copy-done.2
  33.0 0.0 copy-done.3
  33.0 0.0 copy-done.4
  33.1 0.0 copy-done.5
  33.1 2.8 %shard_map.136 = (bf16[128,256]{1,0:T(8,128)(2,1)}, bf16[128,256]{1,0:T(8,128)(2,1)}, bf16[128,256]{1,0:T(8,128)(2,1)}, bf16[128,256]{1,0:T(8,128)(2,1)}, bf16[1...) custom-call(bf16[128,256]{1,0:T(8,128)(2,1)S(1)} %bitcast.16, bf16[128,256]{1,0:T(8,128)(2,1)S(1)} %bitcast.18, ...), custom_call_target="tpu_custom_call" | custom-call | tf_op jit(solution)/shard_map/pallas_call | solution.py:724
Async XLA Ops:
  0.6 32.4 %copy-start = (bf16[1,128,256]{2,1,0:T(8,128)(2,1)S(1)}, bf16[1,128,256]{2,1,0:T(8,128)(2,1)}, u32[]{:S(2)}) copy-start(bf16[1,128,256]{2,1,0:T(8,128)(2,1)} %param.8) | copy-start | bytes 196612
  0.6 32.4 %copy-start.1 = (bf16[1,128,256]{2,1,0:T(8,128)(2,1)S(1)}, bf16[1,128,256]{2,1,0:T(8,128)(2,1)}, u32[]{:S(2)}) copy-start(bf16[1,128,256]{2,1,0:T(8,128)(2,1)} %param.9) | copy-start | bytes 196612
  0.7 32.4 %copy-start.2 = (bf16[1,128,256]{2,1,0:T(8,128)(2,1)S(1)}, bf16[1,128,256]{2,1,0:T(8,128)(2,1)}, u32[]{:S(2)}) copy-start(bf16[1,128,256]{2,1,0:T(8,128)(2,1)} %param.10) | copy-start | bytes 196612
  0.7 32.4 %copy-start.3 = (bf16[1,128,256]{2,1,0:T(8,128)(2,1)S(1)}, bf16[1,128,256]{2,1,0:T(8,128)(2,1)}, u32[]{:S(2)}) copy-start(bf16[1,128,256]{2,1,0:T(8,128)(2,1)} %param.12) | copy-start | bytes 196612
  0.7 32.4 %copy-start.4 = (bf16[1,128,256]{2,1,0:T(8,128)(2,1)S(1)}, bf16[1,128,256]{2,1,0:T(8,128)(2,1)}, u32[]{:S(2)}) copy-start(bf16[1,128,256]{2,1,0:T(8,128)(2,1)} %param.13) | copy-start | bytes 196612
  0.7 32.4 %copy-start.5 = (bf16[1,128,256]{2,1,0:T(8,128)(2,1)S(1)}, bf16[1,128,256]{2,1,0:T(8,128)(2,1)}, u32[]{:S(2)}) copy-start(bf16[1,128,256]{2,1,0:T(8,128)(2,1)} %param.15) | copy-start | bytes 196612

commit v4 on v3

--- a/solution.py
+++ b/solution.py
@@ -444,9 +444,10 @@
     pl.when(is_owner)(lambda: pl.semaphore_wait(barrier, ROW - 1 + ROWS - 1))
     pl.when(is_adder)(lambda: pl.semaphore_wait(barrier, ROW - 1 + 2 * ROWS - 1))
     pl.when(jnp.logical_not(is_owner | is_adder))(lambda: pl.semaphore_wait(barrier, 4))
-    for p in (0, 1):
-        direct = jnp.logical_not(mine[p] | adds[1 - p])
-        pl.when(direct)(lambda p=p: to_owner(p).start())
+    direct = [jnp.logical_not(mine[p] | adds[1 - p]) for p in (0, 1)]
+    waits = (d == 1) & jnp.logical_not(is_owner)
+    pl.when(direct[0])(lambda: to_owner(0).start())
+    pl.when(direct[1] & jnp.logical_not(waits))(lambda: to_owner(1).start())
 
     for p in (0, 1):
         term[p] = jnp.broadcast_to(bonus_terms(parts[p]), (8, PAIR))
@@ -481,13 +482,15 @@
     for p in (0, 1):
         pl.when(jnp.logical_not(adds[p]))(lambda p=p: to_adder(p).start())
 
-    for p in (0, 1):
-        got = local_rest(parts[p])
+    rests = [local_rest(parts[p]) for p in (0, 1)]
+    for p, got in enumerate(rests):
         for ref, values in zip((narrow, deep, wide), got):
             for i, value in enumerate(values):
                 ref[p, i] = value
         for i, line in enumerate(got[3]):
             state[p, BACK + 8 + i : BACK + 9 + i] = line
+
+    pl.when(direct[1] & waits)(lambda: to_owner(1).start())
 
     @pl.when(is_adder)
     def _():

time: 36.2 us -> 36.8 us (1.017)
  no operation moved by 1% of the time
where the time goes in v4:
time: 36.8 us; the launch traced here: 36.2 us
  Pallas kernels  35.4 us (96%)
  between operations  0.74 us (2%)
    pallas_call x1, Pallas kernels, local(): pl.pallas_call(front_kernel, out_shape=(f32(pairs, BACK + 16, PAIR), bf16...  32.6 us
    pallas_call x1, Pallas kernels, local(): pl.pallas_call(final_kernel, out_shape=(*[bf16(rows, width)] * 6, f32(1,...  2.84 us

profile of v4, /device:TPU:56, one launch (start us, length us, event | category | flops | bytes accessed | tf_op | source)
XLA Modules:
  0.0 36.2 jit_solution(14089613065502518918)
XLA Ops:
  0.6 0.0 copy-start
  0.6 0.0 copy-start.1
  0.7 0.0 copy-start.2
  0.7 0.0 copy-start.3
  0.7 0.0 copy-start.4
  0.7 0.0 copy-start.5
  0.7 32.6 %shard_map.135 = (f32[2,144,128]{2,1,0:T(8,128)S(1)}, bf16[2,14,128,128]{3,2,1,0:T(8,128)(2,1)S(1)}, bf16[2,4,256,128]{3,2,1,0:T(8,128)(2,1)S(1)}, f32[2,7,128,128]{3,2,1,0:T(8,128)S(1)}) custom-call(bf16[128,256]{1,0:T(8,128)(2,1)} %bitcast.15, bf16[128,256]{1,0:T(8,128)(2,1)} %bitcast.17, bf16[128,256]{1,0:T(8,128)(2,1)} %bitcast.19, f32[128,256]{1,0:T(8,128)} %bitcast.27, ...), custom_call_target="tpu_custom_call" | custom-call | tf_op jit(solution)/shard_map/pallas_call | solution.py:696
  33.3 0.0 copy-done
  33.3 0.0 copy-done.1
  33.3 0.0 copy-done.2
  33.3 0.0 copy-done.3
  33.3 0.0 copy-done.4
  33.3 0.0 copy-done.5
  33.3 2.8 %shard_map.136 = (bf16[128,256]{1,0:T(8,128)(2,1)}, bf16[128,256]{1,0:T(8,128)(2,1)}, bf16[128,256]{1,0:T(8,128)(2,1)}, bf16[128,256]{1,0:T(8,128)(2,1)}, bf16[1...) custom-call(bf16[128,256]{1,0:T(8,128)(2,1)S(1)} %bitcast.16, bf16[128,256]{1,0:T(8,128)(2,1)S(1)} %bitcast.18, ...), custom_call_target="tpu_custom_call" | custom-call | tf_op jit(solution)/shard_map/pallas_call | solution.py:727
Async XLA Ops:
  0.6 32.6 %copy-start = (bf16[1,128,256]{2,1,0:T(8,128)(2,1)S(1)}, bf16[1,128,256]{2,1,0:T(8,128)(2,1)}, u32[]{:S(2)}) copy-start(bf16[1,128,256]{2,1,0:T(8,128)(2,1)} %param.8) | copy-start | bytes 196612
  0.6 32.6 %copy-start.1 = (bf16[1,128,256]{2,1,0:T(8,128)(2,1)S(1)}, bf16[1,128,256]{2,1,0:T(8,128)(2,1)}, u32[]{:S(2)}) copy-start(bf16[1,128,256]{2,1,0:T(8,128)(2,1)} %param.9) | copy-start | bytes 196612
  0.7 32.6 %copy-start.2 = (bf16[1,128,256]{2,1,0:T(8,128)(2,1)S(1)}, bf16[1,128,256]{2,1,0:T(8,128)(2,1)}, u32[]{:S(2)}) copy-start(bf16[1,128,256]{2,1,0:T(8,128)(2,1)} %param.10) | copy-start | bytes 196612
  0.7 32.6 %copy-start.3 = (bf16[1,128,256]{2,1,0:T(8,128)(2,1)S(1)}, bf16[1,128,256]{2,1,0:T(8,128)(2,1)}, u32[]{:S(2)}) copy-start(bf16[1,128,256]{2,1,0:T(8,128)(2,1)} %param.12) | copy-start | bytes 196612
  0.7 32.6 %copy-start.4 = (bf16[1,128,256]{2,1,0:T(8,128)(2,1)S(1)}, bf16[1,128,256]{2,1,0:T(8,128)(2,1)}, u32[]{:S(2)}) copy-start(bf16[1,128,256]{2,1,0:T(8,128)(2,1)} %param.13) | copy-start | bytes 196612
  0.7 32.6 %copy-start.5 = (bf16[1,128,256]{2,1,0:T(8,128)(2,1)S(1)}, bf16[1,128,256]{2,1,0:T(8,128)(2,1)}, u32[]{:S(2)}) copy-start(bf16[1,128,256]{2,1,0:T(8,128)(2,1)} %param.15) | copy-start | bytes 196612

commit v5 on v3

--- a/solution.py
+++ b/solution.py
@@ -185,14 +185,15 @@
 def local_message(q, t):
     n = q["z"].shape[0]
     eu = by_head(dot3(cat(t, 0), cat([q["a0"], q["z"]], 1)))
-    fp = by_head(dot3(cat([flip(x) for x in t], 0), cat([q["bf"], q["zd"]], 1)))
+    turned = split(cat([flip(x) for x in t], 0))
+    p_own = by_head(dot3(turned, q["zd"]))
     ml = dot3(flip(q["bf"]), eu)
     row, col = iotas(HEAD, PAIR)
     decay = jnp.where(row == (col & (HEAD - 1)), jnp.exp(-q["end"]), 0.0)
     mt = decay + compact(ml[:, :n])
     lt = compact(ml[:, n:] + dot2(flip(q["kf"]), q["vb"]))
-    ht = compact(flip(dot3(flip(q["a0"]), fp[:, n:]) + dot2(flip(q["r0"]), q["dyb"])))
-    q.update(eu=eu, fp=fp)
+    ht = compact(flip(dot3(flip(q["a0"]), p_own) + dot2(flip(q["r0"]), q["dyb"])))
+    q.update(eu=eu, turned=turned, p_own=p_own)
     return lt, mt, ht
 
 
@@ -213,7 +214,8 @@
 
 def local_rest(q):
     n = q["z"].shape[0]
-    eu, fp = q["eu"], q["fp"]
+    eu = q["eu"]
+    fp = cat([by_head(dot3(q["turned"], q["bf"])), q["p_own"]], 1)
     pk, pr, pa = q["late"]
     upper = gram([pk], [pr, pa])
     row, col = iotas(n, n)
@@ -555,12 +557,19 @@
         tot[0:64] = whole[0]
         tot[64:128] = whole[1]
         tot[128:192] = whole[2]
-        cases = (
-            (lambda xx: (xx > x) & (x == 0), 0, 64),
-            (lambda xx: (xx > x) & (x != 0), 0, 128),
-            (lambda xx: (xx < x) & (x == ROWS - 1), 128, 192),
-            (lambda xx: (xx < x) & (x != ROWS - 1), 64, 192),
-        )
+        def rows_for(here, there):
+            if there > here:
+                return (0, 64) if here == 0 else (0, 128)
+            return (128, 192) if here == ROWS - 1 else (64, 192)
+
+        def rows_cases(act):
+            for here in range(ROWS):
+
+                @pl.when(x == here)
+                def _(here=here):
+                    for there in sorted(range(ROWS), key=lambda r: -abs(r - here)):
+                        if there != here:
+                            act(across(there, *rows_for(here, there), here))
 
         def across(xx, low, high, landing):
             rows = pl.ds(low, high - low)
@@ -568,11 +577,8 @@
                 tot.at[rows], xin.at[landing, rows], xsend.at[xx], xsem.at[landing], at(xx, z)
             )
 
-        for xx in range(ROWS):
-            for when, low, high in cases:
-                pl.when(when(xx))(
-                    lambda xx=xx, low=low, high=high: across(xx, low, high, x).start()
-                )
+        rows_cases(lambda copy: copy.start())
+
         one = [(recv[i, 0:64], recv[i, 64:128], recv[i, 128:192]) for i in range(ROW)]
         before = [None, one[0], pair[0], None, four[0], None, None, None]
         before[3] = joined_states(pair[0], one[2])
@@ -585,28 +591,26 @@
         behind[1] = joined_adjoints(pair[1], four[1])
         behind[0] = joined_adjoints(one[1], behind[1])
 
-        run[...] = jnp.zeros_like(run)
-        for xx in range(ROWS - 1):
-            high = 64 if xx == 0 else 128
-
-            @pl.when(x > xx)
-            def _(xx=xx, high=high):
-                across(xx, 0, high, xx).wait_recv()
-                if xx == 0:
-                    run[0] = xin[0, 0:64]
-                else:
-                    run[0] = dot3(xin[xx, 64:128], spread(run[0])) + xin[xx, 0:64]
-
-        for xx in range(ROWS - 1, 0, -1):
-            low = 128 if xx == ROWS - 1 else 64
-
-            @pl.when(x < xx)
-            def _(xx=xx, low=low):
-                across(xx, low, 192, xx).wait_recv()
-                if xx == ROWS - 1:
-                    run[1] = xin[xx, 128:192]
-                else:
-                    run[1] = dot3(run[1], spread(xin[xx, 64:128])) + xin[xx, 128:192]
+        for here in range(ROWS):
+
+            @pl.when(x == here)
+            def _(here=here):
+                for there in range(ROWS):
+                    if there != here:
+                        across(there, *rows_for(there, here), there).wait_recv()
+                start = end = jnp.zeros((HEAD, PAIR), F32)
+                for there in range(here):
+                    if there:
+                        start = dot3(xin[there, 64:128], spread(start)) + xin[there, 0:64]
+                    else:
+                        start = xin[0, 0:64]
+                for there in range(ROWS - 1, here, -1):
+                    if there < ROWS - 1:
+                        end = dot3(end, spread(xin[there, 64:128])) + xin[there, 128:192]
+                    else:
+                        end = xin[there, 128:192]
+                run[0] = start
+                run[1] = end
 
         sg, gg = run[0], run[1]
         moved = dot3(cat([before[i][1] for i in range(1, ROW)], 0), spread(sg))
@@ -634,11 +638,7 @@
         land[pown] = back[z]
         for give in gives:
             give.wait_send()
-        for xx in range(ROWS):
-            for when, low, high in cases:
-                pl.when(when(xx))(
-                    lambda xx=xx, low=low, high=high: across(xx, low, high, x).wait_send()
-                )
+        rows_cases(lambda copy: copy.wait_send())
 
     for p in (0, 1):
 

time: 36.2 us -> 36.2 us (level)
  no operation moved by 1% of the time
where the time goes in v5:
time: 36.2 us; the launch traced here: 35.9 us
  Pallas kernels  35.2 us (97%)
  between operations  0.74 us (2%)
    pallas_call x1, Pallas kernels, local(): pl.pallas_call(front_kernel, out_shape=(f32(pairs, BACK + 16, PAIR), bf16...  32.3 us
    pallas_call x1, Pallas kernels, local(): pl.pallas_call(final_kernel, out_shape=(*[bf16(rows, width)] * 6, f32(1,...  2.84 us

profile of v5, /device:TPU:56, one launch (start us, length us, event | category | flops | bytes accessed | tf_op | source)
XLA Modules:
  0.0 35.9 jit_solution(1393211004509195873)
XLA Ops:
  0.6 0.0 copy-start
  0.6 0.0 copy-start.1
  0.7 0.0 copy-start.2
  0.7 0.0 copy-start.3
  0.7 0.0 copy-start.4
  0.7 0.0 copy-start.5
  0.7 32.3 %shard_map.135 = (f32[2,144,128]{2,1,0:T(8,128)S(1)}, bf16[2,14,128,128]{3,2,1,0:T(8,128)(2,1)S(1)}, bf16[2,4,256,128]{3,2,1,0:T(8,128)(2,1)S(1)}, f32[2,7,128,128]{3,2,1,0:T(8,128)S(1)}) custom-call(bf16[128,256]{1,0:T(8,128)(2,1)} %bitcast.15, bf16[128,256]{1,0:T(8,128)(2,1)} %bitcast.17, bf16[128,256]{1,0:T(8,128)(2,1)} %bitcast.19, f32[128,256]{1,0:T(8,128)} %bitcast.27, ...), custom_call_target="tpu_custom_call" | custom-call | tf_op jit(solution)/shard_map/pallas_call | solution.py:693
  33.0 0.0 copy-done
  33.0 0.0 copy-done.1
  33.0 0.0 copy-done.2
  33.0 0.0 copy-done.3
  33.1 0.0 copy-done.4
  33.1 0.0 copy-done.5
  33.1 2.8 %shard_map.136 = (bf16[128,256]{1,0:T(8,128)(2,1)}, bf16[128,256]{1,0:T(8,128)(2,1)}, bf16[128,256]{1,0:T(8,128)(2,1)}, bf16[128,256]{1,0:T(8,128)(2,1)}, bf16[1...) custom-call(bf16[128,256]{1,0:T(8,128)(2,1)S(1)} %bitcast.16, bf16[128,256]{1,0:T(8,128)(2,1)S(1)} %bitcast.18, ...), custom_call_target="tpu_custom_call" | custom-call | tf_op jit(solution)/shard_map/pallas_call | solution.py:724
Async XLA Ops:
  0.6 32.4 %copy-start = (bf16[1,128,256]{2,1,0:T(8,128)(2,1)S(1)}, bf16[1,128,256]{2,1,0:T(8,128)(2,1)}, u32[]{:S(2)}) copy-start(bf16[1,128,256]{2,1,0:T(8,128)(2,1)} %param.8) | copy-start | bytes 196612
  0.6 32.4 %copy-start.1 = (bf16[1,128,256]{2,1,0:T(8,128)(2,1)S(1)}, bf16[1,128,256]{2,1,0:T(8,128)(2,1)}, u32[]{:S(2)}) copy-start(bf16[1,128,256]{2,1,0:T(8,128)(2,1)} %param.9) | copy-start | bytes 196612
  0.7 32.4 %copy-start.2 = (bf16[1,128,256]{2,1,0:T(8,128)(2,1)S(1)}, bf16[1,128,256]{2,1,0:T(8,128)(2,1)}, u32[]{:S(2)}) copy-start(bf16[1,128,256]{2,1,0:T(8,128)(2,1)} %param.10) | copy-start | bytes 196612
  0.7 32.4 %copy-start.3 = (bf16[1,128,256]{2,1,0:T(8,128)(2,1)S(1)}, bf16[1,128,256]{2,1,0:T(8,128)(2,1)}, u32[]{:S(2)}) copy-start(bf16[1,128,256]{2,1,0:T(8,128)(2,1)} %param.12) | copy-start | bytes 196612
  0.7 32.4 %copy-start.4 = (bf16[1,128,256]{2,1,0:T(8,128)(2,1)S(1)}, bf16[1,128,256]{2,1,0:T(8,128)(2,1)}, u32[]{:S(2)}) copy-start(bf16[1,128,256]{2,1,0:T(8,128)(2,1)} %param.13) | copy-start | bytes 196612
  0.7 32.4 %copy-start.5 = (bf16[1,128,256]{2,1,0:T(8,128)(2,1)S(1)}, bf16[1,128,256]{2,1,0:T(8,128)(2,1)}, u32[]{:S(2)}) copy-start(bf16[1,128,256]{2,1,0:T(8,128)(2,1)} %param.15) | copy-start | bytes 196612

commit v6 on v5

--- a/solution.py
+++ b/solution.py
@@ -38,7 +38,7 @@
         wide = cat([cat([yh, yl], 1 - axis)] * 2, axis)
         both = mm(cat([xh, xl], 1), wide, dims)
         return both[:, :PAIR] + both[:, PAIR:]
-    return mm(cat([xh, xl], 1), cat([yh, yh], axis), dims) + mm(xh, yl, dims)
+    return mm(cat([xh, xl, xh], 1), cat([yh, yh, yl], axis), dims)
 
 
 def dot2(x, y, dims=NN):

time: 36.2 us -> 36.2 us (level)
  no operation moved by 1% of the time
where the time goes in v6:
time: 36.2 us; the launch traced here: 36 us
  Pallas kernels  35.2 us (97%)
  between operations  0.74 us (2%)
    pallas_call x1, Pallas kernels, local(): pl.pallas_call(front_kernel, out_shape=(f32(pairs, BACK + 16, PAIR), bf16...  32.3 us
    pallas_call x1, Pallas kernels, local(): pl.pallas_call(final_kernel, out_shape=(*[bf16(rows, width)] * 6, f32(1,...  2.85 us

profile of v6, /device:TPU:56, one launch (start us, length us, event | category | flops | bytes accessed | tf_op | source)
XLA Modules:
  0.0 36.0 jit_solution(3305783697512462738)
XLA Ops:
  0.6 0.0 copy-start
  0.6 0.0 copy-start.1
  0.7 0.0 copy-start.2
  0.7 0.0 copy-start.3
  0.7 0.0 copy-start.4
  0.7 0.0 copy-start.5
  0.7 32.3 %shard_map.135 = (f32[2,144,128]{2,1,0:T(8,128)S(1)}, bf16[2,14,128,128]{3,2,1,0:T(8,128)(2,1)S(1)}, bf16[2,4,256,128]{3,2,1,0:T(8,128)(2,1)S(1)}, f32[2,7,128,128]{3,2,1,0:T(8,128)S(1)}) custom-call(bf16[128,256]{1,0:T(8,128)(2,1)} %bitcast.15, bf16[128,256]{1,0:T(8,128)(2,1)} %bitcast.17, bf16[128,256]{1,0:T(8,128)(2,1)} %bitcast.19, f32[128,256]{1,0:T(8,128)} %bitcast.27, ...), custom_call_target="tpu_custom_call" | custom-call | tf_op jit(solution)/shard_map/pallas_call | solution.py:693
  33.0 0.0 copy-done
  33.1 0.0 copy-done.1
  33.1 0.0 copy-done.2
  33.1 0.0 copy-done.3
  33.1 0.0 copy-done.4
  33.1 0.0 copy-done.5
  33.1 2.8 %shard_map.136 = (bf16[128,256]{1,0:T(8,128)(2,1)}, bf16[128,256]{1,0:T(8,128)(2,1)}, bf16[128,256]{1,0:T(8,128)(2,1)}, bf16[128,256]{1,0:T(8,128)(2,1)}, bf16[1...) custom-call(bf16[128,256]{1,0:T(8,128)(2,1)S(1)} %bitcast.16, bf16[128,256]{1,0:T(8,128)(2,1)S(1)} %bitcast.18, ...), custom_call_target="tpu_custom_call" | custom-call | tf_op jit(solution)/shard_map/pallas_call | solution.py:724
Async XLA Ops:
  0.6 32.4 %copy-start = (bf16[1,128,256]{2,1,0:T(8,128)(2,1)S(1)}, bf16[1,128,256]{2,1,0:T(8,128)(2,1)}, u32[]{:S(2)}) copy-start(bf16[1,128,256]{2,1,0:T(8,128)(2,1)} %param.8) | copy-start | bytes 196612
  0.6 32.4 %copy-start.1 = (bf16[1,128,256]{2,1,0:T(8,128)(2,1)S(1)}, bf16[1,128,256]{2,1,0:T(8,128)(2,1)}, u32[]{:S(2)}) copy-start(bf16[1,128,256]{2,1,0:T(8,128)(2,1)} %param.9) | copy-start | bytes 196612
  0.7 32.4 %copy-start.2 = (bf16[1,128,256]{2,1,0:T(8,128)(2,1)S(1)}, bf16[1,128,256]{2,1,0:T(8,128)(2,1)}, u32[]{:S(2)}) copy-start(bf16[1,128,256]{2,1,0:T(8,128)(2,1)} %param.10) | copy-start | bytes 196612
  0.7 32.4 %copy-start.3 = (bf16[1,128,256]{2,1,0:T(8,128)(2,1)S(1)}, bf16[1,128,256]{2,1,0:T(8,128)(2,1)}, u32[]{:S(2)}) copy-start(bf16[1,128,256]{2,1,0:T(8,128)(2,1)} %param.12) | copy-start | bytes 196612
  0.7 32.4 %copy-start.4 = (bf16[1,128,256]{2,1,0:T(8,128)(2,1)S(1)}, bf16[1,128,256]{2,1,0:T(8,128)(2,1)}, u32[]{:S(2)}) copy-start(bf16[1,128,256]{2,1,0:T(8,128)(2,1)} %param.13) | copy-start | bytes 196612
  0.7 32.4 %copy-start.5 = (bf16[1,128,256]{2,1,0:T(8,128)(2,1)S(1)}, bf16[1,128,256]{2,1,0:T(8,128)(2,1)}, u32[]{:S(2)}) copy-start(bf16[1,128,256]{2,1,0:T(8,128)(2,1)} %param.15) | copy-start | bytes 196612

commit v7 on v3

--- a/solution.py
+++ b/solution.py
@@ -256,8 +256,7 @@
 
     def apply(mat, y):
         mh, ml = split(mat)
-        both = mm(mh, cat(y, 1))
-        return by_head(both[:, :PAIR] + both[:, PAIR:] + mm(ml, y[0]))
+        return by_head(mm(cat([mh, ml, mh], 1), cat([y[0], y[0], y[1]], 0)))
 
     ra = apply(fwd, by)
     bk = apply(bwd, ry)

time: 36.2 us -> 36.4 us (level)
  no operation moved by 1% of the time
where the time goes in v7:
time: 36.4 us; the launch traced here: 36.2 us
  Pallas kernels  35.4 us (97%)
  between operations  0.74 us (2%)
    pallas_call x1, Pallas kernels, local(): pl.pallas_call(front_kernel, out_shape=(f32(pairs, BACK + 16, PAIR), bf16...  32.3 us
    pallas_call x1, Pallas kernels, local(): pl.pallas_call(final_kernel, out_shape=(*[bf16(rows, width)] * 6, f32(1,...  3.11 us

profile of v7, /device:TPU:56, one launch (start us, length us, event | category | flops | bytes accessed | tf_op | source)
XLA Modules:
  0.0 36.2 jit_solution(1739525534324501093)
XLA Ops:
  0.6 0.0 copy-start
  0.6 0.0 copy-start.1
  0.7 0.0 copy-start.2
  0.7 0.0 copy-start.3
  0.7 0.0 copy-start.4
  0.7 0.0 copy-start.5
  0.7 32.3 %shard_map.135 = (f32[2,144,128]{2,1,0:T(8,128)S(1)}, bf16[2,14,128,128]{3,2,1,0:T(8,128)(2,1)S(1)}, bf16[2,4,256,128]{3,2,1,0:T(8,128)(2,1)S(1)}, f32[2,7,128,128]{3,2,1,0:T(8,128)S(1)}) custom-call(bf16[128,256]{1,0:T(8,128)(2,1)} %bitcast.15, bf16[128,256]{1,0:T(8,128)(2,1)} %bitcast.17, bf16[128,256]{1,0:T(8,128)(2,1)} %bitcast.19, f32[128,256]{1,0:T(8,128)} %bitcast.27, ...), custom_call_target="tpu_custom_call" | custom-call | tf_op jit(solution)/shard_map/pallas_call | solution.py:692
  33.0 0.0 copy-done
  33.0 0.0 copy-done.1
  33.0 0.0 copy-done.2
  33.0 0.0 copy-done.3
  33.0 0.0 copy-done.4
  33.1 0.0 copy-done.5
  33.1 3.1 %shard_map.136 = (bf16[128,256]{1,0:T(8,128)(2,1)}, bf16[128,256]{1,0:T(8,128)(2,1)}, bf16[128,256]{1,0:T(8,128)(2,1)}, bf16[128,256]{1,0:T(8,128)(2,1)}, bf16[1...) custom-call(bf16[128,256]{1,0:T(8,128)(2,1)S(1)} %bitcast.16, bf16[128,256]{1,0:T(8,128)(2,1)S(1)} %bitcast.18, ...), custom_call_target="tpu_custom_call" | custom-call | tf_op jit(solution)/shard_map/pallas_call | solution.py:723
Async XLA Ops:
  0.6 32.4 %copy-start = (bf16[1,128,256]{2,1,0:T(8,128)(2,1)S(1)}, bf16[1,128,256]{2,1,0:T(8,128)(2,1)}, u32[]{:S(2)}) copy-start(bf16[1,128,256]{2,1,0:T(8,128)(2,1)} %param.8) | copy-start | bytes 196612
  0.6 32.4 %copy-start.1 = (bf16[1,128,256]{2,1,0:T(8,128)(2,1)S(1)}, bf16[1,128,256]{2,1,0:T(8,128)(2,1)}, u32[]{:S(2)}) copy-start(bf16[1,128,256]{2,1,0:T(8,128)(2,1)} %param.9) | copy-start | bytes 196612
  0.7 32.4 %copy-start.2 = (bf16[1,128,256]{2,1,0:T(8,128)(2,1)S(1)}, bf16[1,128,256]{2,1,0:T(8,128)(2,1)}, u32[]{:S(2)}) copy-start(bf16[1,128,256]{2,1,0:T(8,128)(2,1)} %param.10) | copy-start | bytes 196612
  0.7 32.4 %copy-start.3 = (bf16[1,128,256]{2,1,0:T(8,128)(2,1)S(1)}, bf16[1,128,256]{2,1,0:T(8,128)(2,1)}, u32[]{:S(2)}) copy-start(bf16[1,128,256]{2,1,0:T(8,128)(2,1)} %param.12) | copy-start | bytes 196612
  0.7 32.4 %copy-start.4 = (bf16[1,128,256]{2,1,0:T(8,128)(2,1)S(1)}, bf16[1,128,256]{2,1,0:T(8,128)(2,1)}, u32[]{:S(2)}) copy-start(bf16[1,128,256]{2,1,0:T(8,128)(2,1)} %param.13) | copy-start | bytes 196612
  0.7 32.4 %copy-start.5 = (bf16[1,128,256]{2,1,0:T(8,128)(2,1)S(1)}, bf16[1,128,256]{2,1,0:T(8,128)(2,1)}, u32[]{:S(2)}) copy-start(bf16[1,128,256]{2,1,0:T(8,128)(2,1)} %param.15) | copy-start | bytes 196612
